TPU v7x, 256 devices: a whole 4x4x8 slice. The times are simulated.
256 devices in a mesh: row: 16 (over z, y_hi), col: 16 (over y_lo, x, core).
Axes of the slice: x: 4, y: 4 (y_hi: 2, y_lo: 2; y = y_hi * 2 + y_lo), z: 8, core: 2. Of those that a mesh axis runs over, the one named last changes fastest.
Arguments:
- tokens: bfloat16 [1, 256, 256, 512], P(None, 'row', 'col'), may hold values from -6 to 6
- cotangent: bfloat16 [1, 256, 256, 512], P(None, 'row', 'col'), may hold values from -16 to 16
- regions: int32 [1, 256, 256], P(None, 'row', 'col'), may hold values from 0 to 3
- qkv_weight: bfloat16 [512, 1536], replicated, may hold values from -0.25 to 0.25
- query_bias: float32 [512], replicated, may hold values from -3 to 3
- value_bias: float32 [512], replicated, may hold values from -3 to 3
- logit_scale: float32 [16], replicated, may hold values from 1.5 to 5.3
- bias_network_entry_weight: float32 [2, 512], replicated, may hold values from -4 to 4
- bias_network_entry_bias: float32 [512], replicated, may hold values from -3 to 3
- bias_network_exit_weight: float32 [512, 16], replicated, may hold values from -0.25 to 0.25
- proj_weight: bfloat16 [512, 512], replicated, may hold values from -0.25 to 0.25
- proj_bias: float32 [512], replicated, may hold values from -3 to 3
- attn_gain: float32 [512], replicated, may hold values from 0.5 to 1.5
- attn_shift: float32 [512], replicated, may hold values from -3 to 3
- hidden_weight: bfloat16 [512, 2048], replicated, may hold values from -0.25 to 0.25
- hidden_bias: float32 [2048], replicated, may hold values from -3 to 3
- output_weight: bfloat16 [2048, 512], replicated, may hold values from -0.125 to 0.125
- output_bias: float32 [512], replicated, may hold values from -3 to 3
- mlp_gain: float32 [512], replicated, may hold values from 0.5 to 1.5
Outputs:
- grad_tokens: bfloat16 [1, 256, 256, 512], P(None, 'row', 'col')
- gradient_query_key_value: float32 [786432], P(('row', 'col'))
- grad_proj: float32 [262144], P(('row', 'col'))
- grad_hidden: float32 [1048576], P(('row', 'col'))
- grad_output: float32 [1048576], P(('row', 'col'))
- grad_vectors: float32 [8, 512], replicated
- grad_hidden_bias: float32 [2048], replicated
- grad_logit_scale: float32 [16], replicated
- grad_bias_mlp_in: float32 [3, 512], replicated
- grad_bias_mlp_out: float32 [512, 16], replicated
All inputs are finite; a program needn't handle non-finite values.
Results may differ from a plain program's by a relative error of at most 0.015.
The roundings to bfloat16 on the way count: a program that leaves them out, or rounds other values in their place, can miss the bound.
Values may be sent and summed in bfloat16 or wider, within the bound.
No kernel may reach another device: no remote copies, remote signals or barrier semaphores. Data moves between devices by JAX's collectives and lax.ppermute only.
A program may use at most 256 MiB of HBM per device.

v0:
```python
import math

import jax
import jax.numpy as jnp
from jax import lax
from jax.experimental import pallas as pl
from jax.experimental.pallas import tpu as pltpu
from jax.sharding import Mesh
from jax.sharding import PartitionSpec as P

WIN = 16
HALF = 8
T = 256
D = 512
HEADS = 16
E = 32
FF = 2048
CH = 512
LANES = 512
ALL = ("z", "yh", "yl", "x", "core")
AXES = (("z", 8), ("yh", 2), ("yl", 2), ("x", 4), ("core", 2))
PLANE = 16
DIRECT = 1536
PLANE_AXES = ALL[1:4]
FACTOR = 1.0 / 256.0
LOG_CAP = math.log(100.0)
TOP = lax.Precision.HIGHEST
BF = jnp.bfloat16
F4 = jnp.float32
PARAMS = pltpu.CompilerParams(vmem_limit_bytes=56 * 1024 * 1024)


def dot(a, b, ca, cb, precision=None):
    return lax.dot_general(
        a, b, (((ca,), (cb,)), ((), ())), precision=precision, preferred_element_type=F4
    )


def split(value, count):
    parts = []
    for _ in range(count):
        parts.append(value.astype(BF).astype(F4))
        value = value - parts[-1]
    return parts


def few_rows(a, b):
    a1, a2, a3 = split(a, 3)
    b1, b2, b3 = split(b, 3)
    left = jnp.concatenate([a1, a1, a2, a2, a1, a3], 0).astype(BF)
    right = jnp.concatenate([b1, b2, b1, b2, b3, b1], 0).astype(BF)
    return dot(left, right, 0, 0)


def few_by_wide(a, b, cb):
    rows = a.shape[0]
    left = jnp.concatenate(split(a, 2), 0).astype(BF)
    high, low = [part.astype(BF) for part in split(b, 2)]
    first, second = dot(left, high, 1, cb), dot(left, low, 1, cb)
    return first[:rows] + (first[rows:] + second[:rows])


def layer_stats(inputs):
    center = inputs - jnp.mean(inputs, -1, keepdims=True)
    inverse = lax.rsqrt(jnp.mean(center * center, -1, keepdims=True) + 1e-05)
    return center * inverse, inverse


def layer_back(upstream, normed, inverse, gain):
    scaled = upstream * gain
    inner = (
        scaled
        - jnp.mean(scaled, -1, keepdims=True)
        - normed * jnp.mean(scaled * normed, -1, keepdims=True)
    )
    return inverse * inner


def col_sum(block):
    return jnp.sum(block, 0, keepdims=True)


def offset_coords():
    lane = lax.broadcasted_iota(jnp.int32, (8, 2 * LANES), 1)
    parity = lane // LANES
    rest = lane - parity * LANES
    pair = rest // 32
    first = 2 * pair + parity
    second = rest - pair * 32
    valid = (first < 31) & (second < 31)

    def logged(index):
        u = (index.astype(F4) - 15.0) / 15.0 * 8.0
        size = jnp.log2(jnp.abs(u) + 1.0) / 3.0
        return jnp.where(u > 0.0, size, jnp.where(u < 0.0, -size, 0.0))

    row = lax.broadcasted_iota(jnp.int32, (8, 2 * LANES), 0)
    coords = jnp.where(
        row == 0, logged(first), jnp.where(row == 1, logged(second), jnp.where(row == 2, 1.0, 0.0))
    )
    return coords, valid


def low_half(shape):
    lane = lax.broadcasted_iota(jnp.int32, shape, len(shape) - 1)
    return lane % 32 < 16


def stack_rows(entry, bias):
    return jnp.concatenate([entry, bias, jnp.zeros((5, entry.shape[1]), F4)], 0)


def spread(ref, block, part, term):
    for lane in range(0, term.shape[1], 128):
        ref[block + lane // 128, pl.ds(part, D, stride=4), :] = term[:, lane : lane + 128]


def joined(ref):
    return jnp.concatenate([ref[b] for b in range(4)], 1)


def ordered(term, core):
    parts = term.reshape(8, PLANE, 2, 8, term.shape[1])
    cut = [parts[:, i, core] for i in range(PLANE)]
    return jnp.concatenate(cut, 0).reshape(-1, term.shape[1])


def paired(term, core):
    parts = term.reshape(8, PLANE, 2, 8, term.shape[1])
    cut = [jnp.concatenate([parts[:4, i, core], parts[4:, i, core]], 2) for i in range(PLANE)]
    return jnp.concatenate(cut, 0).reshape(-1, 2 * term.shape[1])


def paired_lines(term, core, lines):
    parts = term.reshape(4, 2, PLANE, 2, 8, term.shape[1])[:, lines]
    cut = [jnp.concatenate([parts[:2, i, core], parts[2:, i, core]], 2) for i in range(PLANE)]
    return jnp.concatenate(cut, 0).reshape(-1, 2 * term.shape[1])


def split_cores(core, first, second, keep_ref, send_ref, start):
    rows = pl.ds(start, first.shape[0])
    keep_ref[rows, :] = jnp.where(core == 0, first, second).astype(BF)
    send_ref[rows, :] = jnp.where(core == 0, second, first).astype(BF)


def line_kernel(early_ref, late_ref, line_ref, out_ref):
    early = early_ref[...]
    late = jnp.sum(late_ref[...].astype(F4), 0)
    half = D // 2
    for z in range(8):
        rows = slice(8 * z, 8 * z + 8)
        spot = 64 + 8 * (z % 4)
        direct = early[spot : spot + 8, z // 4 * half : (z // 4 + 1) * half]
        spot = 64 + 8 * (z // 2 % 2)
        turned = late[spot : spot + 8, z // 4 * half : (z // 4 + 1) * half]
        turned = jnp.where(line_ref[0] % 2 == z % 2, turned, 0.0)
        output = jnp.concatenate([direct, turned], 1)
        out_ref[z] = jnp.concatenate([early[rows], output, late[rows]], 0).astype(BF)


def finish_kernel(blocks_ref, hidden_ref, output_ref, qkv_ref, proj_ref):
    total = jnp.sum(blocks_ref[...].astype(F4), 0)
    for r in range(8):
        hidden_ref[r * D : (r + 1) * D] = total[r]
        output_ref[r * D : (r + 1) * D] = total[8 + r]
        qkv_ref[r * 384 : (r + 1) * 384] = total[16 + r, :384]
        proj_ref[r * 128 : (r + 1) * 128] = total[16 + r, 384:]


def unpack_kernel(small_ref, others_ref, vectors_ref, hidden_ref, logit_ref, first_ref, second_ref):
    rows = [pl.ds(c, 32, stride=4) for c in range(4)]
    total = jnp.concatenate([small_ref[r, :] + others_ref[r, :] for r in rows], 1)
    vectors_ref[...] = total[:8]
    for c in range(4):
        hidden_ref[c * D : (c + 1) * D] = total[8 + c]
    first_ref[...] = total[12:15]
    second_ref[...] = total[15:31]
    logit_ref[...] = total[31, :HEADS]


def bias_kernel(entry_ref, mid_ref, exit_ref, wide_ref, squashed_ref, scratch):
    coords, _ = offset_coords()
    before = few_rows(stack_rows(entry_ref[...], mid_ref[...]), coords)
    hidden = jnp.maximum(before, 0.0)
    squashed = jax.nn.sigmoid(few_by_wide(exit_ref[...], hidden, 0))
    squashed_ref[...] = squashed
    table = 16.0 * squashed
    even, odd = table[:, :LANES], table[:, LANES:]
    low = low_half((HEADS, LANES))
    for c in range(WIN):
        scratch[c] = jnp.where(
            low,
            pltpu.roll(even, (c - 15) % LANES, 1),
            pltpu.roll(odd, (c + 1) % LANES, 1),
        )
    for h in range(HEADS):
        wide_ref[h] = scratch[:, h, :]


def forward_kernel(
    tokens_ref, cotangent_ref, down_ref, right_ref, diag_ref, regions_ref, wide_ref,
    qkv_ref, qbias_ref, vbias_ref, logit_ref,
    proj_ref, pbias_ref, again_ref, ashift_ref,
    hidden_ref, hbias_ref, output_ref, obias_ref, mgain_ref, core_ref, line_ref,
    x_ref, probs_ref, qunit_ref, kunit_ref, inverse_ref, value_ref, att_ref,
    normed_ref, ainverse_ref, gmiddle_ref, vectors_ref, hsum_ref, keep_ref, send_ref,
    qlow_s, klow_s, act_s, slope_s, ghidden_s, goutput_s,
    whidden_s, woutput_s, x_s, probs_s, qunit_s, kunit_s, value_s, att_s, normed_s, gmiddle_s, sems,
):
    loads = [
        pltpu.make_async_copy(hidden_ref, whidden_s, sems.at[0]),
        pltpu.make_async_copy(output_ref, woutput_s, sems.at[1]),
    ]
    for load in loads:
        load.start()
    stores = []

    def store(scratch, ref):
        stores.append(pltpu.make_async_copy(scratch, ref, sems.at[2 + len(stores)]))
        stores[-1].start()

    def assemble(own_ref, i):
        top = jnp.concatenate([own_ref[0, HALF:, HALF:], right_ref[i]], 1)
        bottom = jnp.concatenate([down_ref[i], diag_ref[i]], 1)
        return jnp.concatenate([top, bottom], 0).reshape(T, D)

    x = assemble(tokens_ref, 0)
    x_s[...] = x.T
    store(x_s, x_ref)
    mixed = dot(x, qkv_ref[...], 1, 0)
    q = (mixed[:, :D] + qbias_ref[...]).T
    k = mixed[:, D : 2 * D].T
    value_s[...] = (mixed[:, 2 * D :] + vbias_ref[...]).T.astype(BF)
    for index, (raw, unit_ref, low_s) in enumerate(
        ((q, qunit_s, qlow_s), (k, kunit_s, klow_s))
    ):
        split = raw.reshape(HEADS, E, T)
        inverse = lax.rsqrt(jnp.sum(split * split, 1, keepdims=True) + 1e-06)
        inverse_ref[index] = inverse
        unit = (split * inverse).reshape(D, T)
        unit_ref[...] = unit
        low_s[...] = unit.astype(BF)
    store(qunit_s, qunit_ref)
    store(kunit_s, kunit_ref)
    store(value_s, value_ref)
    own_row = lax.broadcasted_iota(jnp.int32, (WIN, T), 0)
    token = lax.broadcasted_iota(jnp.int32, (WIN, T), 1)
    pick = jnp.where(token % WIN == own_row, 1.0, 0.0).astype(BF)
    by_row = dot(regions_ref[0].astype(F4).astype(BF), pick, 1, 0)
    region_row = col_sum(jnp.where(token // WIN == own_row, by_row, 0.0))
    region_col = jnp.broadcast_to(region_row, (8, T)).T[:, :1]
    allowed = region_col == region_row

    def head(h, carry):
        at = pl.ds(pl.multiple_of(h * E, E), E)
        scale = jnp.exp(jnp.minimum(jnp.full((1, T), logit_ref[h], F4), LOG_CAP))
        cosine = dot(klow_s[at, :], qlow_s[at, :], 0, 0)
        wide = wide_ref[h]
        rolled = [wide] + [pltpu.roll(wide, LANES - 16 * p, 1) for p in range(1, 8)]
        bias = jnp.concatenate(
            [
                rolled[(15 - r) % 8][:, (15 - r) // 8 * 128 : (15 - r) // 8 * 128 + T]
                for r in range(WIN)
            ],
            0,
        )
        logits = jnp.where(allowed, scale * cosine + bias, -1000000000.0)
        powers = jnp.exp(logits - jnp.max(logits, 0, keepdims=True))
        probs = powers / jnp.sum(powers, 0, keepdims=True)
        probs_s[h] = probs
        pltpu.make_async_copy(probs_s.at[h], probs_ref.at[h], sems.at[9]).start()
        att_s[at, :] = dot(value_s[at, :], probs.astype(BF), 1, 0).astype(BF)
        return carry

    lax.fori_loop(0, HEADS, head, 0, unroll=2)

    store(att_s, att_ref)
    projected = dot(att_s[...], proj_ref[...], 0, 0) + pbias_ref[...]
    attn_normed, attn_inverse = layer_stats(projected)
    normed_s[...] = attn_normed
    store(normed_s, normed_ref)
    ainverse_ref[...] = attn_inverse
    middle = x.astype(F4) + (attn_normed * again_ref[...] + ashift_ref[...])
    middle_low = middle.astype(BF)
    for load in loads:
        load.wait()
    emitted = jnp.zeros((T, D), F4)
    for c in range(0, FF, CH):
        cut = slice(c, c + CH)
        before = dot(middle_low, whidden_s[:, cut], 1, 0) + hbias_ref[:, cut]
        cumulative = 0.5 * (1.0 + lax.erf(before * (1.0 / math.sqrt(2.0))))
        density = jnp.exp(-0.5 * before * before) * (1.0 / math.sqrt(2.0 * math.pi))
        slope_s[:, cut] = cumulative + before * density
        act = (before * cumulative).astype(BF)
        act_s[:, cut] = act
        emitted += dot(act, woutput_s[cut, :], 1, 0)
    normed, inverse = layer_stats(emitted + obias_ref[...])
    incoming = assemble(cotangent_ref, 1).astype(F4)
    grad_emitted = layer_back(incoming, normed, inverse, mgain_ref[...])
    emitted_low = grad_emitted.astype(BF)
    vectors_ref[0:1, :] = col_sum(grad_emitted) * FACTOR
    vectors_ref[1:2, :] = col_sum(incoming * normed) * FACTOR
    vectors_ref[2:3, :] = col_sum(incoming) * FACTOR
    grad_middle = incoming
    for c in range(0, FF, CH):
        cut = slice(c, c + CH)
        grad_act = dot(emitted_low, woutput_s[cut, :], 1, 1)
        grad_before = grad_act * slope_s[:, cut]
        hsum_ref[:, cut] = col_sum(grad_before) * FACTOR
        before_low = grad_before.astype(BF)
        goutput_s[cut, :] = dot(act_s[:, cut], emitted_low, 0, 0) * FACTOR
        spread(ghidden_s, 0, c // CH, dot(middle_low, before_low, 0, 0) * FACTOR)
        grad_middle += dot(before_low, whidden_s[:, cut], 1, 1)
    gmiddle_s[...] = grad_middle
    store(gmiddle_s, gmiddle_ref)
    core = core_ref[0]
    term = joined(ghidden_s)
    split_cores(core, ordered(term, 0), ordered(term, 1), keep_ref, send_ref, 0)
    term = goutput_s[...]
    even = line_ref[0] % 2 == 0
    half = D // 2
    direct, turned = term[:, :half], term[:, half:]
    split_cores(core, paired(direct, 0), paired(direct, 1), keep_ref, send_ref, FF // 2)
    halves = [[paired_lines(turned, k, lines) for lines in range(2)] for k in range(2)]
    near = [jnp.where(even, a, b) for a, b in halves]
    far = [jnp.where(even, b, a) for a, b in halves]
    split_cores(core, *near, keep_ref, send_ref, DIRECT)
    split_cores(core, *far, keep_ref, send_ref, DIRECT + 256)
    pltpu.make_async_copy(probs_s, probs_ref, sems.at[9]).wait()
    for done in stores:
        done.wait()


def middle_kernel(
    att_ref, normed_ref, ainverse_ref, gmiddle_ref, proj_ref, again_ref,
    gatt_ref, gproj_ref, vectors_ref,
):
    grad_middle = gmiddle_ref[...]
    attn_normed = normed_ref[...]
    grad_projected = layer_back(grad_middle, attn_normed, ainverse_ref[...], again_ref[...])
    projected_low = grad_projected.astype(BF)
    gatt_ref[...] = dot(proj_ref[...], projected_low, 1, 1).astype(BF)
    vectors_ref[0:1, :] = col_sum(grad_projected) * FACTOR
    vectors_ref[1:2, :] = col_sum(grad_middle * attn_normed) * FACTOR
    vectors_ref[2:3, :] = col_sum(grad_middle) * FACTOR
    grad_proj = dot(att_ref[...], projected_low, 1, 0) * FACTOR
    for c in range(4):
        gproj_ref[pl.ds(c, D, stride=4), :] = grad_proj[:, c * 128 : (c + 1) * 128]


def window_kernel(mixed_ref, gmiddle_ref, qkv_ref, own_ref, down_ref, right_ref, diag_ref):
    window = gmiddle_ref[...] + dot(mixed_ref[...], qkv_ref[...], 1, 1)
    window = window.astype(BF).reshape(WIN, WIN, D)
    own_ref[...] = window[:HALF, :HALF]
    right_ref[...] = window[:HALF, HALF:]
    down_ref[...] = window[HALF:, :HALF]
    diag_ref[...] = window[HALF:, HALF:]


def heads_kernel(
    probs_ref, qunit_ref, kunit_ref, inverse_ref, value_ref, gatt_s,
    logit_ref,
    mixed_ref, sums_ref, wide_s,
    qlow_s, klow_s, gmixed_s,
):
    qlow_s[...] = qunit_ref[...].astype(BF)
    klow_s[...] = kunit_ref[...].astype(BF)

    def head(h, carry):
        at = pl.ds(pl.multiple_of(h * E, E), E)
        kat = pl.ds(pl.multiple_of(h * E + D, E), E)
        vat = pl.ds(pl.multiple_of(h * E + 2 * D, E), E)
        scale = jnp.exp(jnp.minimum(jnp.full((1, T), logit_ref[h], F4), LOG_CAP))
        qlow, klow, gatt = qlow_s[at, :], klow_s[at, :], gatt_s[at, :]
        probs = probs_ref[h]
        grad_probs = dot(value_ref[at, :], gatt, 0, 0)
        gmixed_s[vat, :] = dot(gatt, probs.astype(BF), 1, 1)
        grad_scores = probs * (grad_probs - jnp.sum(probs * grad_probs, 0, keepdims=True))
        cosine = dot(klow, qlow, 0, 0)
        live = jnp.full((1, T), logit_ref[h], F4) < LOG_CAP
        total = jnp.sum(jnp.sum(grad_scores * cosine, 0, keepdims=True), 1, keepdims=True)
        term = jnp.where(live, total * scale * FACTOR, 0.0)
        lane = lax.broadcasted_iota(jnp.int32, (1, T), 1)
        carry = carry + jnp.where(lane == h, term, 0.0)
        grad_cosine = (grad_scores * scale).astype(BF)
        for index, (part, unit_ref, where) in enumerate(
            (
                (dot(klow, grad_cosine, 1, 0), qunit_ref, at),
                (dot(qlow, grad_cosine, 1, 1), kunit_ref, kat),
            )
        ):
            unit = unit_ref[at, :]
            gmixed_s[where, :] = inverse_ref[index, h] * (
                part - unit * jnp.sum(unit * part, 0, keepdims=True)
            )
        wide = None
        for p in range(8):
            first = grad_scores[(15 - p) * 16 : (16 - p) * 16]
            second = grad_scores[(7 - p) * 16 : (8 - p) * 16]
            blank = jnp.zeros((WIN, 128), F4)
            placed = jnp.concatenate(
                [first[:, :128], first[:, 128:] + second[:, :128], second[:, 128:], blank], 1
            )
            if p:
                placed = pltpu.roll(placed, 16 * p, 1)
            wide = placed if wide is None else wide + placed
        wide_s[h] = wide
        return carry

    logits = lax.fori_loop(0, HEADS, head, jnp.zeros((1, T), F4), unroll=2)
    sums_ref[2:3, :] = jnp.concatenate([logits, jnp.zeros((1, D - T), F4)], 1)

    ones = jnp.ones((8, T), F4)
    sums_ref[0:1, :] = few_by_wide(ones, gmixed_s[0:D, :], 1)[:1] * FACTOR
    sums_ref[1:2, :] = few_by_wide(ones, gmixed_s[2 * D :, :], 1)[:1] * FACTOR
    mixed_ref[...] = gmixed_s[...].astype(BF).T


def grads_kernel(x_ref, mixed_ref, gproj_ref, core_ref, keep_ref, send_ref, grads_s):
    mixed = mixed_ref[...]
    for c in range(4):
        cut = slice(c * 384, (c + 1) * 384)
        spread(grads_s, 0, c, dot(x_ref[...], mixed[:, cut], 1, 0) * FACTOR)
    grads = jnp.concatenate([grads_s[0], grads_s[1], grads_s[2], gproj_ref[...]], 1)
    split_cores(core_ref[0], ordered(grads, 0), ordered(grads, 1), keep_ref, send_ref, 0)


def table_kernel(
    entry_ref, mid_ref, exit_ref, squashed_ref, wide_s,
    sums_ref, attn_ref, mlp_ref, hsum_ref,
    small_ref,
    small_s,
):
    small_s[0:2, :] = sums_ref[0:2, :]
    small_s[2:5, :] = attn_ref[...]
    small_s[5:8, :] = mlp_ref[...]
    for c in range(0, FF, D):
        small_s[8 + c // D : 9 + c // D, :] = hsum_ref[:, c : c + D]
    small_s[31:32, :] = sums_ref[2:3, :]
    low = low_half((HEADS, LANES))
    even = jnp.zeros((HEADS, LANES), F4)
    odd = jnp.zeros((HEADS, LANES), F4)
    for c in range(WIN):
        part = wide_s[:, c, :]
        even += pltpu.roll(jnp.where(low, part, 0.0), (15 - c) % LANES, 1)
        odd += pltpu.roll(jnp.where(low, 0.0, part), (LANES - 1 - c) % LANES, 1)
    coords, valid = offset_coords()
    squashed = squashed_ref[...]
    table = jnp.concatenate([even, odd], 1) * 16.0 * squashed * (1.0 - squashed) * FACTOR
    table = jnp.where(valid[:1], table, 0.0)
    before = few_rows(stack_rows(entry_ref[...], mid_ref[...]), coords)
    small_s[15:31, :] = few_by_wide(table, jnp.maximum(before, 0.0), 1)
    grad_pos = jnp.where(before > 0.0, few_rows(exit_ref[...], table), 0.0)
    small_s[12:15, :] = few_by_wide(coords, grad_pos, 1)[:3]
    small = small_s[...]
    for c in range(4):
        small_ref[pl.ds(c, 32, stride=4), :] = small[:, c * 128 : (c + 1) * 128]


def shape(*dims, dtype=F4):
    return jax.ShapeDtypeStruct(dims, dtype)


def vmem(*dims, dtype=F4):
    return pltpu.VMEM(dims, dtype)


def whole(count, scalar=(), far=()):
    def space(i):
        return pltpu.SMEM if i in scalar else pl.ANY if i in far else pltpu.VMEM

    return [pl.BlockSpec(memory_space=space(i)) for i in range(count)]


def device_index(row, col):
    return (row % 16) * 16 + col % 16


def moved(block, rows, cols):
    route = [
        (device_index(r, c), device_index(r + rows, c + cols)) for r in range(16) for c in range(16)
    ]
    return lax.ppermute(block, ALL, route)


def swapped(block):
    return lax.ppermute(block, "core", [(0, 1), (1, 0)])


def joint(keep, got):
    return (keep.astype(F4) + got.astype(F4)).astype(BF)


def exchanged(blocks, axes):
    return lax.all_to_all(blocks, axes, 0, 0)


def rounds(small, steps):
    for axis, size, step in steps:
        small = small + lax.ppermute(small, axis, [(i, i ^ step) for i in range(size)])
    return small


def across(block):
    return lax.ppermute(block, "z", [(i, i ^ 1) for i in range(8)])


def cost(us):
    return pl.CostEstimate(flops=int(us * 5e8), bytes_accessed=int(us * 2e6), transcendentals=0)


def local(
    tokens, cotangent, regions, qkv_weight, query_bias, value_bias, logit_scale,
    entry_weight, entry_bias, exit_weight, proj_weight, proj_bias, attn_gain, attn_shift,
    hidden_weight, hidden_bias, output_weight, output_bias, mlp_gain,
):
    row = lambda v: v.reshape(1, -1)

    def strip(rows, cols):
        return jnp.concatenate([tokens[:, rows, cols], cotangent[:, rows, cols]], 0)

    head, tail = slice(0, HALF), slice(HALF, WIN)
    down = moved(strip(head, tail), -1, 0)
    right = moved(strip(tail, head), 0, -1)
    diag = moved(strip(head, head), -1, -1)
    exit_turned = exit_weight.T
    wide, squashed = pl.pallas_call(
        bias_kernel,
        out_shape=(
            shape(HEADS, WIN, LANES), shape(HEADS, 2 * LANES),
        ),
        in_specs=whole(3),
        out_specs=tuple(whole(2)),
        scratch_shapes=[vmem(WIN, HEADS, LANES)],
        compiler_params=PARAMS,
        cost_estimate=cost(5),
        name="bias",
    )(entry_weight, row(entry_bias), exit_turned)
    core = lax.axis_index("core").astype(jnp.int32).reshape(1)
    line = lax.axis_index("z").astype(jnp.int32).reshape(1)
    (
        x, probs, qunit, kunit, inverse, value, att, normed, ainverse, gmiddle,
        mlp_vectors, hidden_sum, keep, send,
    ) = pl.pallas_call(
        forward_kernel,
        out_shape=(
            shape(D, T, dtype=BF), shape(HEADS, T, T), shape(D, T), shape(D, T),
            shape(2, HEADS, 1, T), shape(D, T, dtype=BF), shape(D, T, dtype=BF),
            shape(T, D), shape(T, 1), shape(T, D), shape(3, D), shape(1, FF),
            shape(FF, D, dtype=BF), shape(FF, D, dtype=BF),
        ),
        in_specs=whole(22, (10, 20, 21), (15, 17)),
        out_specs=tuple(whole(14, (), (0, 1, 2, 3, 5, 6, 7, 9))),
        scratch_shapes=[
            vmem(D, T, dtype=BF), vmem(D, T, dtype=BF), vmem(T, FF, dtype=BF), vmem(T, FF),
            vmem(4, FF, 128), vmem(FF, D),
            vmem(D, FF, dtype=BF), vmem(FF, D, dtype=BF), vmem(D, T, dtype=BF),
            vmem(HEADS, T, T), vmem(D, T), vmem(D, T), vmem(D, T, dtype=BF),
            vmem(D, T, dtype=BF), vmem(T, D), vmem(T, D), pltpu.SemaphoreType.DMA((10,)),
        ],
        compiler_params=PARAMS,
        cost_estimate=cost(17),
        name="forward",
    )(
        tokens, cotangent, down, right, diag, regions, wide,
        qkv_weight, row(query_bias), row(value_bias), logit_scale,
        proj_weight, row(proj_bias), row(attn_gain), row(attn_shift),
        hidden_weight, row(hidden_bias), output_weight, row(output_bias), row(mlp_gain), core, line,
    )
    got = swapped(send)
    grad_att, grad_proj, attn_vectors = pl.pallas_call(
        middle_kernel,
        out_shape=(shape(D, T, dtype=BF), shape(FF, 128), shape(3, D)),
        in_specs=whole(6),
        out_specs=tuple(whole(3)),
        compiler_params=PARAMS,
        cost_estimate=cost(0.5),
        name="middle",
    )(att, normed, ainverse, gmiddle, proj_weight, row(attn_gain))
    early = jnp.concatenate(
        [
            joint(keep[:1024], got[:1024]).reshape(PLANE, 64, D),
            joint(keep[1024:DIRECT], got[1024:DIRECT]).reshape(PLANE, 32, D),
        ],
        1,
    )
    far = joint(keep[DIRECT + 256 :], got[DIRECT + 256 :])
    near = joint(keep[DIRECT : DIRECT + 256], got[DIRECT : DIRECT + 256])
    early, far, near, grad_att = lax.optimization_barrier((early, far, near, grad_att))
    far = across(far)
    early = exchanged(early, PLANE_AXES)
    mixed, token_sums, wide = pl.pallas_call(
        heads_kernel,
        out_shape=(shape(T, 3 * D, dtype=BF), shape(3, D), shape(HEADS, WIN, LANES)),
        in_specs=whole(7, (6,)),
        out_specs=tuple(whole(3)),
        scratch_shapes=[vmem(D, T, dtype=BF), vmem(D, T, dtype=BF), vmem(3 * D, T)],
        compiler_params=PARAMS,
        cost_estimate=cost(0.5),
        name="heads",
    )(probs, qunit, kunit, inverse, value, grad_att, logit_scale)
    small = pl.pallas_call(
        table_kernel,
        out_shape=shape(128, 128),
        in_specs=whole(9),
        out_specs=whole(1)[0],
        scratch_shapes=[vmem(32, D)],
        compiler_params=PARAMS,
        cost_estimate=cost(0.5),
        name="table",
    )(
        entry_weight, row(entry_bias), exit_turned, squashed, wide,
        token_sums, attn_vectors, mlp_vectors, hidden_sum,
    )
    mixed, far, small = lax.optimization_barrier((mixed, far, small))
    keep, send = pl.pallas_call(
        grads_kernel,
        out_shape=(shape(FF // 2, D, dtype=BF), shape(FF // 2, D, dtype=BF)),
        in_specs=whole(4, (3,)),
        out_specs=tuple(whole(2)),
        scratch_shapes=[vmem(3, FF, 128)],
        compiler_params=PARAMS,
        cost_estimate=cost(0.5),
        name="grads",
    )(x, mixed, grad_proj, core)
    got = swapped(send)
    small = small + swapped(small)
    mixed, small = lax.optimization_barrier((mixed, small))
    small = rounds(small, (("z", 8, 1),))
    back_own, back_down, back_right, back_diag = pl.pallas_call(
        window_kernel,
        out_shape=tuple(shape(HALF, HALF, D, dtype=BF) for _ in range(4)),
        in_specs=whole(3),
        out_specs=tuple(whole(4)),
        compiler_params=PARAMS,
        cost_estimate=cost(2),
        name="window",
    )(mixed, gmiddle, qkv_weight)
    got, keep, early, small, back_own, back_down, back_right, back_diag = lax.optimization_barrier(
        (got, keep, early, small, back_own, back_down, back_right, back_diag)
    )
    early = jnp.sum(early.astype(F4), 0)
    late = jnp.concatenate(
        [joint(keep, got).reshape(PLANE, 64, D), joint(near, far).reshape(PLANE, 16, D)], 1
    )
    late = exchanged(late, PLANE_AXES)
    small = rounds(small, (("z", 8, 2), ("z", 8, 4), ("x", 4, 1)))
    from_above = moved(back_down, 1, 0)
    from_left = moved(back_right, 0, 1)
    from_diag = moved(back_diag, 1, 1)
    grad_tokens = jnp.concatenate(
        [
            jnp.concatenate([from_diag, from_above], 1),
            jnp.concatenate([from_left, back_own], 1),
        ],
        0,
    )[None]
    late, small, grad_tokens = lax.optimization_barrier((late, small, grad_tokens))
    small = rounds(small, (("x", 4, 2), ("yl", 2, 1)))
    blocks = pl.pallas_call(
        line_kernel,
        out_shape=shape(8, 24, D, dtype=BF),
        in_specs=whole(3, (2,)),
        out_specs=whole(1)[0],
        compiler_params=PARAMS,
        cost_estimate=cost(2),
        name="line",
    )(early, late, line)
    sum_hidden, sum_output, sum_qkv, sum_proj = pl.pallas_call(
        finish_kernel,
        out_shape=(shape(8 * D), shape(8 * D), shape(8 * 384), shape(8 * 128)),
        in_specs=whole(1),
        out_specs=tuple(whole(4)),
        compiler_params=PARAMS,
        cost_estimate=cost(1),
        name="finish",
    )(exchanged(blocks, "z"))
    small, sum_hidden, sum_output, sum_qkv, sum_proj = lax.optimization_barrier(
        (small, sum_hidden, sum_output, sum_qkv, sum_proj)
    )
    others = lax.ppermute(small, "yh", [(0, 1), (1, 0)])
    vectors, hidden_total, logit_total, first, second = pl.pallas_call(
        unpack_kernel,
        out_shape=(shape(8, D), shape(FF), shape(HEADS), shape(3, D), shape(HEADS, D)),
        in_specs=whole(2),
        out_specs=tuple(whole(5)),
        compiler_params=PARAMS,
        cost_estimate=cost(1),
        name="unpack",
    )(small, others)
    return (
        grad_tokens,
        sum_qkv,
        sum_proj,
        sum_hidden,
        sum_output,
        vectors,
        hidden_total,
        logit_total,
        first,
        second.T,
    )


def solution(mesh):
    fine = Mesh(mesh.devices.reshape([n for _, n in AXES]), ALL)
    tile = P(None, ("z", "yh"), ("yl", "x", "core"))
    return jax.shard_map(
        local,
        mesh=fine,
        in_specs=(tile, tile, tile) + (P(),) * 16,
        out_specs=(tile,) + (P(ALL),) * 4 + (P(),) * 5,
        check_vma=False,
    )
```

profile of v0, /device:TPU:32, one launch (start us, length us, event | category | flops | bytes accessed | tf_op | source)
XLA Modules:
  0.0 138.5 jit_solution(1227979356617679722)
XLA Ops:
  0.6 1.0 fusion
  1.7 2.8 %collective-permute-start = (bf16[2,8,8,512]{3,2,1,0:T(8,128)(2,1)S(1)}, bf16[2,8,8,512]{3,2,1,0:T(8,128)(2,1)S(1)}, u32[]{:S(2)}, u32[]{:S(2)}) collective-permute-start(bf16[2,8,8,512]{3,2,1,0:T(8,128)(2,1)S(1)} %pad_maximum_fusion.2), channel_id=1, source_target_pairs={{0,240},{1,241},{2,242},{3,243},{4,244},{5,245},{6,246},{7,247},{8... | collective-permute-start | bytes 393224 | tf_op jit(solution)/shard_map/ppermute | solution.py:483
  4.5 2.1 %collective-permute-start.1 = (bf16[2,8,8,512]{3,2,1,0:T(8,128)(2,1)S(1)}, bf16[2,8,8,512]{3,2,1,0:T(8,128)(2,1)S(1)}, u32[]{:S(2)}, u32[]{:S(2)}) collective-permute-start(bf16[2,8,8,512]{3,2,1,0:T(8,128)(2,1)S(1)} %pad_maximum_fusion.3), channel_id=1, source_target_pairs={{0,15},{1,0},{2,1},{3,2},{4,3},{5,4},{6,5},{7,6},{8,7},{9,8},{10,9... | collective-permute-start | bytes 393224 | tf_op jit(solution)/shard_map/ppermute | solution.py:483
  6.7 1.4 %collective-permute-start.2 = (bf16[2,8,8,512]{3,2,1,0:T(8,128)(2,1)S(1)}, bf16[2,8,8,512]{3,2,1,0:T(8,128)(2,1)S(1)}, u32[]{:S(2)}, u32[]{:S(2)}) collective-permute-start(bf16[2,8,8,512]{3,2,1,0:T(8,128)(2,1)S(1)} %pad_maximum_fusion.4), channel_id=1, source_target_pairs={{0,255},{1,240},{2,241},{3,242},{4,243},{5,244},{6,245},{7,246},{8... | collective-permute-start | bytes 393224 | tf_op jit(solution)/shard_map/ppermute | solution.py:483
  8.1 2.8 %bias.1 = (f32[16,16,512]{2,1,0:T(8,128)}, f32[16,1024]{1,0:T(8,128)}) custom-call(f32[2,512]{1,0:T(2,128)} %entry_ref.3, f32[1,512]{1,0:T(1,128)} %bitcast.34, f32[16,512]{1,0:T(8,128)} %bitcast.25), custom_call_target="tpu_custom_call" | custom-call | flops 2500000000 | bytes 10000000 | tf_op jit(solution)/shard_map/bias/pallas_call | solution.py:527
  10.9 2.7 %collective-permute-done.2.diag_ref = bf16[2,8,8,512]{3,2,1,0:T(8,128)(2,1)S(1)} collective-permute-done((bf16[2,8,8,512]{3,2,1,0:T(8,128)(2,1)S(1)}, bf16[2,8,8,512]{3,2,1,0:T(8,128)(2,1)S(1)}, u32[]{:S(2)}, u32[]{:S(2)}) %collective-permute-start.2) | collective-permute-done | bytes 131104 | tf_op jit(solution)/shard_map/ppermute | solution.py:483
  13.6 0.6 copy-done.9
  14.3 17.6 %forward.1 = (bf16[512,256]{1,0:T(8,128)(2,1)}, f32[16,256,256]{2,1,0:T(8,128)}, f32[512,256]{1,0:T(8,128)}, f32[512,256]{1,0:T(8,128)}, f32[2,16,1,256]{3,2,1,0...) custom-call(bf16[1,16,16,512]{3,2,1,0:T(8,128)(2,1)} %tokens_ref.1, ...), custom_call_target="tpu_custom_call" | custom-call | flops 8499999744 | bytes 34000000 | tf_op jit(solution)/shard_map/forward/pallas_call | solution.py:544
  32.0 3.4 %middle.1 = (bf16[512,256]{1,0:T(8,128)(2,1)}, f32[2048,128]{1,0:T(8,128)}, f32[3,512]{1,0:T(4,128)}) custom-call(bf16[512,256]{1,0:T(8,128)(2,1)} %get-tuple-element.81.att_ref, f32[256,512]{1,0:T(8,128)} %get-tuple-element.82.normed_ref, f32[256,1]{1,0:T(8,128)} %get-tuple-element.83.ainverse_ref, f32[256,512]{1,0:T(8,128)} %get-tuple-element.84.gmiddle_ref, ...), custom_call_target="tpu_custom_call" | custom-call | flops 250000000 | bytes 1000000 | tf_op jit(solution)/shard_map/middle/pallas_call | solution.py:571
  35.4 1.0 collective-permute-done.3
  36.4 1.2 add_convert_fusion.2
  37.9 1.3 pad_maximum_fusion
  39.3 7.1 %all-to-all-start = ((bf16[16,96,512]{2,1,0:T(8,128)(2,1)}), bf16[16,96,512]{2,1,0:T(8,128)(2,1)S(1)}, u32[]{:S(2)}, u32[]{:S(2)}) async-start(bf16[16,96,512]{2,1,0:T(8,128)(2,1)} %pad_maximum_fusion), calls=%async_computation | async-start | bytes 3145728 | tf_op jit(solution)/shard_map/all_to_all | solution.py:495
  46.4 2.8 %collective-permute-start.4 = (bf16[256,512]{1,0:T(8,128)(2,1)S(1)}, bf16[256,512]{1,0:T(8,128)(2,1)S(1)}, u32[]{:S(2)}, u32[]{:S(2)}) collective-permute-start(bf16[256,512]{1,0:T(8,128)(2,1)S(1)} %get-tuple-element.88), channel_id=1, source_target_pairs={{0,32},{32,0},{64,96},{96,64},{128,160},{160,128},{192,224},{224,1... | collective-permute-start | bytes 786440 | tf_op jit(solution)/shard_map/ppermute | solution.py:505
  49.2 10.1 %heads.1 = (bf16[256,1536]{1,0:T(8,128)(2,1)}, f32[3,512]{1,0:T(4,128)}, f32[16,16,512]{2,1,0:T(8,128)}) custom-call(f32[16,256,256]{2,1,0:T(8,128)} %get-tuple-element.74.probs_ref, f32[512,256]{1,0:T(8,128)} %get-tuple-element.75.qunit_ref, f32[512,256]{1,0:T(8,128)} %get-tuple-element.76.kunit_ref, f32[2,16,1,256]{3,2,1,0:T(1,128)} %get-tuple-element.77.inverse_ref, ...), custom_call_target="tpu_custom_call" | custom-call | flops 250000000 | bytes 1000000 | tf_op jit(solution)/shard_map/heads/pallas_call | solution.py:592
  59.2 3.7 %table.1 = f32[128,128]{1,0:T(8,128)} custom-call(f32[2,512]{1,0:T(2,128)} %entry_ref.3, f32[1,512]{1,0:T(1,128)} %bitcast.35, f32[16,512]{1,0:T(8,128)} %bitcast.26, f32[16,1024]{1,0:T(8,128)} %get-tuple-element.89.squashed_ref, f32[16,16,512]{2,1,0:T(8,128)} %get-tuple-element.90.wide_s, f32[3,512]{1,0:T(4,128)} %get-tuple-element.91.sums_ref, ...), custom_call_target="tpu_custom_call" | custom-call | flops 250000000 | bytes 1000000 | tf_op jit(solution)/shard_map/table/pallas_call | solution.py:602
  62.9 3.9 %grads.1 = (bf16[1024,512]{1,0:T(8,128)(2,1)}, bf16[1024,512]{1,0:T(8,128)(2,1)}) custom-call(bf16[512,256]{1,0:T(8,128)(2,1)} %get-tuple-element.73.x_ref, bf16[256,1536]{1,0:T(8,128)(2,1)} %get-tuple-element.102.mixed_ref, f32[2048,128]{1,0:T(8,128)} %get-tuple-element.96.gproj_ref, s32[1]{0:T(128)} %bitcast.10.core_ref), custom_call_target="tpu_custom_call" | custom-call | flops 250000000 | bytes 1000000 | tf_op jit(solution)/shard_map/grads/pallas_call | solution.py:616
  66.8 0.5 collective-permute-start.6
  67.4 1.8 %collective-permute-done.6 = f32[128,128]{1,0:T(8,128)S(1)} collective-permute-done((f32[128,128]{1,0:T(8,128)S(1)}, f32[128,128]{1,0:T(8,128)S(1)}, u32[]{:S(2)}, u32[]{:S(2)}) %collective-permute-start.6) | collective-permute-done | bytes 65568 | tf_op jit(solution)/shard_map/ppermute | solution.py:487
  69.2 0.5 collective-permute-start.7
  69.7 3.1 %window.1 = (bf16[8,8,512]{2,1,0:T(8,128)(2,1)}, bf16[8,8,512]{2,1,0:T(8,128)(2,1)}, bf16[8,8,512]{2,1,0:T(8,128)(2,1)}, bf16[8,8,512]{2,1,0:T(8,128)(2,1)}) custom-call(bf16[256,1536]{1,0:T(8,128)(2,1)} %get-tuple-element.102.mixed_ref, f32[256,512]{1,0:T(8,128)} %get-tuple-element.84.gmiddle_ref, bf16[512,1536]{1,0:T(8,128)(2,1)} %qkv_ref.3), custom_call_target="tpu_custom_call" | custom-call | flops 1000000000 | bytes 4000000 | tf_op jit(solution)/shard_map/window/pallas_call | solution.py:630
  72.7 0.9 collective-permute-done.7
  73.7 1.5 %add_convert_fusion = bf16[1024,512]{1,0:T(8,128)(2,1)S(1)} fusion(bf16[1024,512]{1,0:T(8,128)(2,1)} %collective-permute-done.5, bf16[1024,512]{1,0:T(8,128)(2,1)S(1)} %copy-done.2), kind=kLoop, calls=%fused_computation.1 | loop fusion | flops 2097152 | bytes 3145728 | tf_op jit(solution)/shard_map/convert_element_type | solution.py:491
  75.2 1.2 pad_maximum_fusion.1
  76.4 7.0 %all-to-all-start.1 = ((bf16[16,80,512]{2,1,0:T(8,128)(2,1)}), bf16[16,80,512]{2,1,0:T(8,128)(2,1)S(1)}, u32[]{:S(2)}, u32[]{:S(2)}) async-start(bf16[16,80,512]{2,1,0:T(8,128)(2,1)} %pad_maximum_fusion.1), calls=%async_computation.1 | async-start | bytes 2621440 | tf_op jit(solution)/shard_map/all_to_all | solution.py:495
  83.5 2.7 %collective-permute-start.8 = (f32[128,128]{1,0:T(8,128)S(1)}, f32[128,128]{1,0:T(8,128)S(1)}, u32[]{:S(2)}, u32[]{:S(2)}) collective-permute-start(f32[128,128]{1,0:T(8,128)S(1)} %add.44), channel_id=1, source_target_pairs={{0,64},{32,96},{64,0},{96,32},{128,192},{160,224},{192,128},{224,1... | collective-permute-start | bytes 196616 | tf_op jit(solution)/shard_map/ppermute | solution.py:500
  86.1 2.2 %collective-permute-start.11 = (bf16[8,8,512]{2,1,0:T(8,128)(2,1)S(1)}, bf16[8,8,512]{2,1,0:T(8,128)(2,1)S(1)}, u32[]{:S(2)}, u32[]{:S(2)}) collective-permute-start(bf16[8,8,512]{2,1,0:T(8,128)(2,1)S(1)} %copy-done.12), channel_id=1, source_target_pairs={{0,17},{1,18},{2,19},{3,20},{4,21},{5,22},{6,23},{7,24},{8,25},{9,... | collective-permute-start | bytes 196616 | tf_op jit(solution)/shard_map/ppermute | solution.py:483
  88.3 1.2 collective-permute-start.12
  89.6 1.0 collective-permute-start.13
  90.6 4.2 %collective-permute-start.9 = (f32[128,128]{1,0:T(8,128)S(1)}, f32[128,128]{1,0:T(8,128)S(1)}, u32[]{:S(2)}, u32[]{:S(2)}) collective-permute-start(f32[128,128]{1,0:T(8,128)S(1)} %add.47), channel_id=1, source_target_pairs={{0,128},{32,160},{64,192},{96,224},{128,0},{160,32},{192,64},{224,... | collective-permute-start | bytes 196616 | tf_op jit(solution)/shard_map/ppermute | solution.py:500
  94.8 0.9 convert_reduce_fusion.early_ref
  95.8 3.5 %collective-permute-done.9 = f32[128,128]{1,0:T(8,128)S(1)} collective-permute-done((f32[128,128]{1,0:T(8,128)S(1)}, f32[128,128]{1,0:T(8,128)S(1)}, u32[]{:S(2)}, u32[]{:S(2)}) %collective-permute-start.9) | collective-permute-done | bytes 65568 | tf_op jit(solution)/shard_map/ppermute | solution.py:500
  99.3 1.6 %collective-permute-start.10 = (f32[128,128]{1,0:T(8,128)S(1)}, f32[128,128]{1,0:T(8,128)S(1)}, u32[]{:S(2)}, u32[]{:S(2)}) collective-permute-start(f32[128,128]{1,0:T(8,128)S(1)} %add.48), channel_id=1, source_target_pairs={{0,2},{2,0},{4,6},{6,4},{1,3},{3,1},{5,7},{7,5},{8,10},{10,8},{12,... | collective-permute-start | bytes 196616 | tf_op jit(solution)/shard_map/ppermute | solution.py:500
  100.8 1.6 %collective-permute-done.13 = bf16[8,8,512]{2,1,0:T(8,128)(2,1)S(1)} collective-permute-done((bf16[8,8,512]{2,1,0:T(8,128)(2,1)S(1)}, bf16[8,8,512]{2,1,0:T(8,128)(2,1)S(1)}, u32[]{:S(2)}, u32[]{:S(2)}) %collective-permute-start.13) | collective-permute-done | bytes 65568 | tf_op jit(solution)/shard_map/ppermute | solution.py:483
  102.4 0.7 maximum_bitcast_fusion
  103.2 0.5 collective-permute-done.10
  103.7 3.7 %all-to-all-done.1.late_ref = bf16[16,80,512]{2,1,0:T(8,128)(2,1)S(1)} async-done(((bf16[16,80,512]{2,1,0:T(8,128)(2,1)}), bf16[16,80,512]{2,1,0:T(8,128)(2,1)S(1)}, u32[]{:S(2)}, u32[]{:S(2)}) %all-to-all-start.1) | async-done | bytes 1310752 | tf_op jit(solution)/shard_map/all_to_all | solution.py:495
  107.4 1.1 copy-done.1
  108.5 2.3 %line.1 = bf16[8,24,512]{2,1,0:T(8,128)(2,1)} custom-call(f32[96,512]{1,0:T(8,128)} %convert_reduce_fusion.early_ref, bf16[16,80,512]{2,1,0:T(8,128)(2,1)} %copy-done.1, s32[1]{0:T(128)} %bitcast.11.line_ref), custom_call_target="tpu_custom_call" | custom-call | flops 1000000000 | bytes 4000000 | tf_op jit(solution)/shard_map/line/pallas_call | solution.py:660
  110.8 7.4 %all-to-all-start.2 = ((bf16[8,24,512]{2,1,0:T(8,128)(2,1)}), bf16[8,24,512]{2,1,0:T(8,128)(2,1)S(1)}, u32[]{:S(2)}, u32[]{:S(2)}) async-start(bf16[8,24,512]{2,1,0:T(8,128)(2,1)} %line.1), calls=%async_computation.2 | async-start | bytes 393216 | tf_op jit(solution)/shard_map/all_to_all | solution.py:495
  118.1 5.8 %collective-permute-done.14 = f32[128,128]{1,0:T(8,128)S(1)} collective-permute-done((f32[128,128]{1,0:T(8,128)S(1)}, f32[128,128]{1,0:T(8,128)S(1)}, u32[]{:S(2)}, u32[]{:S(2)}) %collective-permute-start.14) | collective-permute-done | bytes 65568 | tf_op jit(solution)/shard_map/ppermute | solution.py:500
  124.0 4.3 %collective-permute-done.15 = f32[128,128]{1,0:T(8,128)S(1)} collective-permute-done((f32[128,128]{1,0:T(8,128)S(1)}, f32[128,128]{1,0:T(8,128)S(1)}, u32[]{:S(2)}, u32[]{:S(2)}) %collective-permute-start.15) | collective-permute-done | bytes 65568 | tf_op jit(solution)/shard_map/ppermute | solution.py:500
  128.3 0.7 copy-done.3
  129.0 1.6 %finish.1 = (f32[4096]{0:T(1024)}, f32[4096]{0:T(1024)}, f32[3072]{0:T(1024)}, f32[1024]{0:T(1024)}) custom-call(bf16[8,24,512]{2,1,0:T(8,128)(2,1)} %copy-done.3), custom_call_target="tpu_custom_call" | custom-call | flops 500000000 | bytes 2000000 | tf_op jit(solution)/shard_map/finish/pallas_call | solution.py:669
  130.6 0.9 collective-permute-start.16
  131.5 4.8 %collective-permute-done.16.others_ref = f32[128,128]{1,0:T(8,128)S(1)} collective-permute-done((f32[128,128]{1,0:T(8,128)S(1)}, f32[128,128]{1,0:T(8,128)S(1)}, u32[]{:S(2)}, u32[]{:S(2)}) %collective-permute-start.16) | collective-permute-done | bytes 65568 | tf_op jit(solution)/shard_map/ppermute | solution.py:681
  136.3 0.6 copy-done.13
  137.0 1.5 %unpack.1 = (f32[8,512]{1,0:T(8,128)}, f32[2048]{0:T(1024)}, f32[16]{0:T(128)}, f32[3,512]{1,0:T(4,128)}, f32[16,512]{1,0:T(8,128)}) custom-call(f32[128,128]{1,0:T(8,128)} %copy-done.5, f32[128,128]{1,0:T(8,128)} %copy-done.13), custom_call_target="tpu_custom_call" | custom-call | flops 500000000 | bytes 2000000 | tf_op jit(solution)/shard_map/unpack/pallas_call | solution.py:682
  (50 shorter events, 0.9 us)
Async XLA Ops:
  1.7 9.2 %collective-permute-start = (bf16[2,8,8,512]{3,2,1,0:T(8,128)(2,1)S(1)}, bf16[2,8,8,512]{3,2,1,0:T(8,128)(2,1)S(1)}, u32[]{:S(2)}, u32[]{:S(2)}) collective-permute-start(bf16[2,8,8,512]{3,2,1,0:T(8,128)(2,1)S(1)} %pad_maximum_fusion.2), channel_id=1, source_target_pairs={{0,240},{1,241},{2,242},{3,243},{4,244},{5,245},{6,246},{7,247},{8... | collective-permute-start | bytes 393224 | tf_op jit(solution)/shard_map/ppermute | solution.py:483
  4.5 6.3 %collective-permute-start.1 = (bf16[2,8,8,512]{3,2,1,0:T(8,128)(2,1)S(1)}, bf16[2,8,8,512]{3,2,1,0:T(8,128)(2,1)S(1)}, u32[]{:S(2)}, u32[]{:S(2)}) collective-permute-start(bf16[2,8,8,512]{3,2,1,0:T(8,128)(2,1)S(1)} %pad_maximum_fusion.3), channel_id=1, source_target_pairs={{0,15},{1,0},{2,1},{3,2},{4,3},{5,4},{6,5},{7,6},{8,7},{9,8},{10,9... | collective-permute-start | bytes 393224 | tf_op jit(solution)/shard_map/ppermute | solution.py:483
  6.7 6.9 %collective-permute-start.2 = (bf16[2,8,8,512]{3,2,1,0:T(8,128)(2,1)S(1)}, bf16[2,8,8,512]{3,2,1,0:T(8,128)(2,1)S(1)}, u32[]{:S(2)}, u32[]{:S(2)}) collective-permute-start(bf16[2,8,8,512]{3,2,1,0:T(8,128)(2,1)S(1)} %pad_maximum_fusion.4), channel_id=1, source_target_pairs={{0,255},{1,240},{2,241},{3,242},{4,243},{5,244},{6,245},{7,246},{8... | collective-permute-start | bytes 393224 | tf_op jit(solution)/shard_map/ppermute | solution.py:483
  10.9 2.7 %copy-start.7 = (bf16[2,8,8,512]{3,2,1,0:T(8,128)(2,1)}, bf16[2,8,8,512]{3,2,1,0:T(8,128)(2,1)S(1)}, u32[]{:S(2)}) copy-start(bf16[2,8,8,512]{3,2,1,0:T(8,128)(2,1)S(1)} %collective-permute-done.down_ref) | copy-start | bytes 393220
  10.9 2.7 %copy-start.8 = (bf16[2,8,8,512]{3,2,1,0:T(8,128)(2,1)}, bf16[2,8,8,512]{3,2,1,0:T(8,128)(2,1)S(1)}, u32[]{:S(2)}) copy-start(bf16[2,8,8,512]{3,2,1,0:T(8,128)(2,1)S(1)} %collective-permute-done.1.right_ref) | copy-start | bytes 393220
  13.6 0.7 copy-start.9
  31.9 5.6 %copy-start = (bf16[2048,512]{1,0:T(8,128)(2,1)S(1)}, bf16[2048,512]{1,0:T(8,128)(2,1)}, u32[]{:S(2)}) copy-start(bf16[2048,512]{1,0:T(8,128)(2,1)} %get-tuple-element.79) | copy-start | bytes 6291460
  31.9 4.5 %collective-permute-start.3 = (bf16[2048,512]{1,0:T(8,128)(2,1)}, bf16[2048,512]{1,0:T(8,128)(2,1)S(1)}, u32[]{:S(2)}, u32[]{:S(2)}) collective-permute-start(bf16[2048,512]{1,0:T(8,128)(2,1)} %get-tuple-element.80), channel_id=1, source_target_pairs={{0,1},{1,0},{2,3},{3,2},{4,5},{5,4},{6,7},{7,6},{8,9},{9,8},{10,11... | collective-permute-start | bytes 6291464 | tf_op jit(solution)/shard_map/ppermute | solution.py:487
  39.3 34.4 %all-to-all-start = ((bf16[16,96,512]{2,1,0:T(8,128)(2,1)}), bf16[16,96,512]{2,1,0:T(8,128)(2,1)S(1)}, u32[]{:S(2)}, u32[]{:S(2)}) async-start(bf16[16,96,512]{2,1,0:T(8,128)(2,1)} %pad_maximum_fusion), calls=%async_computation | async-start | bytes 3145728 | tf_op jit(solution)/shard_map/all_to_all | solution.py:495
  46.4 16.5 %collective-permute-start.4 = (bf16[256,512]{1,0:T(8,128)(2,1)S(1)}, bf16[256,512]{1,0:T(8,128)(2,1)S(1)}, u32[]{:S(2)}, u32[]{:S(2)}) collective-permute-start(bf16[256,512]{1,0:T(8,128)(2,1)S(1)} %get-tuple-element.88), channel_id=1, source_target_pairs={{0,32},{32,0},{64,96},{96,64},{128,160},{160,128},{192,224},{224,1... | collective-permute-start | bytes 786440 | tf_op jit(solution)/shard_map/ppermute | solution.py:505
  62.9 3.9 %copy-start.4 = (f32[128,128]{1,0:T(8,128)S(1)}, f32[128,128]{1,0:T(8,128)}, u32[]{:S(2)}) copy-start(f32[128,128]{1,0:T(8,128)} %table.1) | copy-start | bytes 196612
  66.8 6.9 %collective-permute-start.5 = (bf16[1024,512]{1,0:T(8,128)(2,1)}, bf16[1024,512]{1,0:T(8,128)(2,1)}, u32[]{:S(2)}, u32[]{:S(2)}) collective-permute-start(bf16[1024,512]{1,0:T(8,128)(2,1)} %get-tuple-element.97), channel_id=1, source_target_pairs={{0,1},{1,0},{2,3},{3,2},{4,5},{5,4},{6,7},{7,6},{8,9},{9,8},{10,11... | collective-permute-start | bytes 3145736 | tf_op jit(solution)/shard_map/ppermute | solution.py:487
  66.8 2.4 %collective-permute-start.6 = (f32[128,128]{1,0:T(8,128)S(1)}, f32[128,128]{1,0:T(8,128)S(1)}, u32[]{:S(2)}, u32[]{:S(2)}) collective-permute-start(f32[128,128]{1,0:T(8,128)S(1)} %copy-done.4), channel_id=1, source_target_pairs={{0,1},{1,0},{2,3},{3,2},{4,5},{5,4},{6,7},{7,6},{8,9},{9,8},{10,11... | collective-permute-start | bytes 196616 | tf_op jit(solution)/shard_map/ppermute | solution.py:487
  67.4 6.3 %copy-start.2 = (bf16[1024,512]{1,0:T(8,128)(2,1)S(1)}, bf16[1024,512]{1,0:T(8,128)(2,1)}, u32[]{:S(2)}) copy-start(bf16[1024,512]{1,0:T(8,128)(2,1)} %get-tuple-element.107) | copy-start | bytes 3145732
  69.2 4.5 %collective-permute-start.7 = (f32[128,128]{1,0:T(8,128)S(1)}, f32[128,128]{1,0:T(8,128)S(1)}, u32[]{:S(2)}, u32[]{:S(2)}) collective-permute-start(f32[128,128]{1,0:T(8,128)S(1)} %add.43), channel_id=1, source_target_pairs={{0,32},{32,0},{64,96},{96,64},{128,160},{160,128},{192,224},{224,1... | collective-permute-start | bytes 196616 | tf_op jit(solution)/shard_map/ppermute | solution.py:500
  75.2 10.9 %copy-start.12 = (bf16[8,8,512]{2,1,0:T(8,128)(2,1)S(1)}, bf16[8,8,512]{2,1,0:T(8,128)(2,1)}, u32[]{:S(2)}) copy-start(bf16[8,8,512]{2,1,0:T(8,128)(2,1)} %get-tuple-element.112) | copy-start | bytes 196612
  75.2 13.1 %copy-start.11 = (bf16[8,8,512]{2,1,0:T(8,128)(2,1)S(1)}, bf16[8,8,512]{2,1,0:T(8,128)(2,1)}, u32[]{:S(2)}) copy-start(bf16[8,8,512]{2,1,0:T(8,128)(2,1)} %get-tuple-element.113) | copy-start | bytes 196612
  75.2 14.4 %copy-start.10 = (bf16[8,8,512]{2,1,0:T(8,128)(2,1)S(1)}, bf16[8,8,512]{2,1,0:T(8,128)(2,1)}, u32[]{:S(2)}) copy-start(bf16[8,8,512]{2,1,0:T(8,128)(2,1)} %get-tuple-element.114) | copy-start | bytes 196612
  76.4 26.0 %copy-start.6 = (bf16[8,8,512]{2,1,0:T(8,128)(2,1)S(1)}, bf16[8,8,512]{2,1,0:T(8,128)(2,1)}, u32[]{:S(2)}) copy-start(bf16[8,8,512]{2,1,0:T(8,128)(2,1)} %get-tuple-element.115) | copy-start | bytes 196612
  76.4 30.9 %all-to-all-start.1 = ((bf16[16,80,512]{2,1,0:T(8,128)(2,1)}), bf16[16,80,512]{2,1,0:T(8,128)(2,1)S(1)}, u32[]{:S(2)}, u32[]{:S(2)}) async-start(bf16[16,80,512]{2,1,0:T(8,128)(2,1)} %pad_maximum_fusion.1), calls=%async_computation.1 | async-start | bytes 2621440 | tf_op jit(solution)/shard_map/all_to_all | solution.py:495
  83.5 7.1 %collective-permute-start.8 = (f32[128,128]{1,0:T(8,128)S(1)}, f32[128,128]{1,0:T(8,128)S(1)}, u32[]{:S(2)}, u32[]{:S(2)}) collective-permute-start(f32[128,128]{1,0:T(8,128)S(1)} %add.44), channel_id=1, source_target_pairs={{0,64},{32,96},{64,0},{96,32},{128,192},{160,224},{192,128},{224,1... | collective-permute-start | bytes 196616 | tf_op jit(solution)/shard_map/ppermute | solution.py:500
  86.1 14.7 %collective-permute-start.11 = (bf16[8,8,512]{2,1,0:T(8,128)(2,1)S(1)}, bf16[8,8,512]{2,1,0:T(8,128)(2,1)S(1)}, u32[]{:S(2)}, u32[]{:S(2)}) collective-permute-start(bf16[8,8,512]{2,1,0:T(8,128)(2,1)S(1)} %copy-done.12), channel_id=1, source_target_pairs={{0,17},{1,18},{2,19},{3,20},{4,21},{5,22},{6,23},{7,24},{8,25},{9,... | collective-permute-start | bytes 196616 | tf_op jit(solution)/shard_map/ppermute | solution.py:483
  88.3 12.5 %collective-permute-start.12 = (bf16[8,8,512]{2,1,0:T(8,128)(2,1)S(1)}, bf16[8,8,512]{2,1,0:T(8,128)(2,1)S(1)}, u32[]{:S(2)}, u32[]{:S(2)}) collective-permute-start(bf16[8,8,512]{2,1,0:T(8,128)(2,1)S(1)} %copy-done.11), channel_id=1, source_target_pairs={{0,16},{1,17},{2,18},{3,19},{4,20},{5,21},{6,22},{7,23},{8,24},{9,... | collective-permute-start | bytes 196616 | tf_op jit(solution)/shard_map/ppermute | solution.py:483
  89.6 12.8 %collective-permute-start.13 = (bf16[8,8,512]{2,1,0:T(8,128)(2,1)S(1)}, bf16[8,8,512]{2,1,0:T(8,128)(2,1)S(1)}, u32[]{:S(2)}, u32[]{:S(2)}) collective-permute-start(bf16[8,8,512]{2,1,0:T(8,128)(2,1)S(1)} %copy-done.10), channel_id=1, source_target_pairs={{0,1},{1,2},{2,3},{3,4},{4,5},{5,6},{6,7},{7,8},{8,9},{9,10},{10,1... | collective-permute-start | bytes 196616 | tf_op jit(solution)/shard_map/ppermute | solution.py:483
  90.6 8.7 %collective-permute-start.9 = (f32[128,128]{1,0:T(8,128)S(1)}, f32[128,128]{1,0:T(8,128)S(1)}, u32[]{:S(2)}, u32[]{:S(2)}) collective-permute-start(f32[128,128]{1,0:T(8,128)S(1)} %add.47), channel_id=1, source_target_pairs={{0,128},{32,160},{64,192},{96,224},{128,0},{160,32},{192,64},{224,... | collective-permute-start | bytes 196616 | tf_op jit(solution)/shard_map/ppermute | solution.py:500
  99.3 4.4 %collective-permute-start.10 = (f32[128,128]{1,0:T(8,128)S(1)}, f32[128,128]{1,0:T(8,128)S(1)}, u32[]{:S(2)}, u32[]{:S(2)}) collective-permute-start(f32[128,128]{1,0:T(8,128)S(1)} %add.48), channel_id=1, source_target_pairs={{0,2},{2,0},{4,6},{6,4},{1,3},{3,1},{5,7},{7,5},{8,10},{10,8},{12,... | collective-permute-start | bytes 196616 | tf_op jit(solution)/shard_map/ppermute | solution.py:500
  107.4 1.1 copy-start.1
  110.8 17.5 %all-to-all-start.2 = ((bf16[8,24,512]{2,1,0:T(8,128)(2,1)}), bf16[8,24,512]{2,1,0:T(8,128)(2,1)S(1)}, u32[]{:S(2)}, u32[]{:S(2)}) async-start(bf16[8,24,512]{2,1,0:T(8,128)(2,1)} %line.1), calls=%async_computation.2 | async-start | bytes 393216 | tf_op jit(solution)/shard_map/all_to_all | solution.py:495
  118.1 5.8 %collective-permute-start.14 = (f32[128,128]{1,0:T(8,128)S(1)}, f32[128,128]{1,0:T(8,128)S(1)}, u32[]{:S(2)}, u32[]{:S(2)}) collective-permute-start(f32[128,128]{1,0:T(8,128)S(1)} %add.49), channel_id=1, source_target_pairs={{0,4},{2,6},{4,0},{6,2},{1,5},{3,7},{5,1},{7,3},{8,12},{10,14},{12... | collective-permute-start | bytes 196616 | tf_op jit(solution)/shard_map/ppermute | solution.py:500
  123.9 4.4 %collective-permute-start.15 = (f32[128,128]{1,0:T(8,128)S(1)}, f32[128,128]{1,0:T(8,128)S(1)}, u32[]{:S(2)}, u32[]{:S(2)}) collective-permute-start(f32[128,128]{1,0:T(8,128)S(1)} %add.50), channel_id=1, source_target_pairs={{0,8},{8,0},{1,9},{9,1},{2,10},{10,2},{3,11},{11,3},{4,12},{12,4},... | collective-permute-start | bytes 196616 | tf_op jit(solution)/shard_map/ppermute | solution.py:500
  128.3 8.0 %copy-start.5 = (f32[128,128]{1,0:T(8,128)}, f32[128,128]{1,0:T(8,128)S(1)}, u32[]{:S(2)}) copy-start(f32[128,128]{1,0:T(8,128)S(1)} %add.51.small_ref) | copy-start | bytes 196612
  128.3 0.7 copy-start.3
  130.6 5.8 %collective-permute-start.16 = (f32[128,128]{1,0:T(8,128)S(1)}, f32[128,128]{1,0:T(8,128)S(1)}, u32[]{:S(2)}, u32[]{:S(2)}) collective-permute-start(f32[128,128]{1,0:T(8,128)S(1)} %add.51.small_ref), channel_id=1, source_target_pairs={{0,16},{16,0},{1,17},{17,1},{2,18},{18,2},{3,19},{19,3},{4,20},{20... | collective-permute-start | bytes 196616 | tf_op jit(solution)/shard_map/ppermute | solution.py:681
  136.3 0.6 copy-start.13
where the time goes:
time: 139 us; the launch traced here: 138 us
  Pallas kernels  49.8 us (36%)
  starting transfers between devices  45.5 us (33%)
  waiting for transfers between devices  30.6 us (22%)
  other arithmetic  7.44 us (5%)
  local copies, waits for them, and re-layouts  4.12 us (3%)
    all_to_all x3, starting transfers between devices, exchanged(): return lax.all_to_all(blocks, axes, 0, 0)  21.4 us
    pallas_call x1, Pallas kernels, local(): pl.pallas_call(forward_kernel, out_shape=(shape(D, T, dtype=BF), shape(HE...  17.6 us
    ppermute x6, waiting for transfers between devices, rounds(): lax.ppermute(small, axis, [(i, i ^ step) for i in range(size)])  14.9 us
    ppermute x6, starting transfers between devices, moved(): return lax.ppermute(block, ALL, route)  10.8 us
    pallas_call x1, Pallas kernels, local(): pl.pallas_call(heads_kernel, out_shape=(shape(T, 3 * D, dtype=BF), shape(...  10.1 us
    ppermute x6, starting transfers between devices, rounds(): lax.ppermute(small, axis, [(i, i ^ step) for i in range(size)])  9.01 us
    ppermute x1, waiting for transfers between devices, local(): others = lax.ppermute(small, 'yh', [(0, 1), (1, 0)])  4.84 us
    ppermute x6, waiting for transfers between devices, moved(): return lax.ppermute(block, ALL, route)  4.32 us
  transfers between devices with their start and end apart: 20, of which 11 were waited for; matrix products, arithmetic and copies ran while one was open for 1% of the time, Pallas kernels for 19%

commit v1 on v0

--- a/solution.py
+++ b/solution.py
@@ -158,21 +158,22 @@
         out_ref[z] = jnp.concatenate([early[rows], output, late[rows]], 0).astype(BF)
 
 
-def finish_kernel(blocks_ref, hidden_ref, output_ref, qkv_ref, proj_ref):
+def finish_kernel(
+    blocks_ref, small_ref, others_ref,
+    hidden_ref, output_ref, qkv_ref, proj_ref,
+    vectors_ref, hbias_ref, logit_ref, first_ref, second_ref,
+):
     total = jnp.sum(blocks_ref[...].astype(F4), 0)
     for r in range(8):
         hidden_ref[r * D : (r + 1) * D] = total[r]
         output_ref[r * D : (r + 1) * D] = total[8 + r]
         qkv_ref[r * 384 : (r + 1) * 384] = total[16 + r, :384]
         proj_ref[r * 128 : (r + 1) * 128] = total[16 + r, 384:]
-
-
-def unpack_kernel(small_ref, others_ref, vectors_ref, hidden_ref, logit_ref, first_ref, second_ref):
     rows = [pl.ds(c, 32, stride=4) for c in range(4)]
     total = jnp.concatenate([small_ref[r, :] + others_ref[r, :] for r in rows], 1)
     vectors_ref[...] = total[:8]
     for c in range(4):
-        hidden_ref[c * D : (c + 1) * D] = total[8 + c]
+        hbias_ref[c * D : (c + 1) * D] = total[8 + c]
     first_ref[...] = total[12:15]
     second_ref[...] = total[15:31]
     logit_ref[...] = total[31, :HEADS]
@@ -266,13 +267,13 @@
         )
         logits = jnp.where(allowed, scale * cosine + bias, -1000000000.0)
         powers = jnp.exp(logits - jnp.max(logits, 0, keepdims=True))
-        probs = powers / jnp.sum(powers, 0, keepdims=True)
+        probs = powers * (1.0 / jnp.sum(powers, 0, keepdims=True))
         probs_s[h] = probs
         pltpu.make_async_copy(probs_s.at[h], probs_ref.at[h], sems.at[9]).start()
         att_s[at, :] = dot(value_s[at, :], probs.astype(BF), 1, 0).astype(BF)
         return carry
 
-    lax.fori_loop(0, HEADS, head, 0, unroll=2)
+    lax.fori_loop(0, HEADS, head, 0, unroll=4)
 
     store(att_s, att_ref)
     projected = dot(att_s[...], proj_ref[...], 0, 0) + pbias_ref[...]
@@ -407,7 +408,7 @@
         wide_s[h] = wide
         return carry
 
-    logits = lax.fori_loop(0, HEADS, head, jnp.zeros((1, T), F4), unroll=2)
+    logits = lax.fori_loop(0, HEADS, head, jnp.zeros((1, T), F4), unroll=4)
     sums_ref[2:3, :] = jnp.concatenate([logits, jnp.zeros((1, D - T), F4)], 1)
 
     ones = jnp.ones((8, T), F4)
@@ -644,7 +645,7 @@
         [joint(keep, got).reshape(PLANE, 64, D), joint(near, far).reshape(PLANE, 16, D)], 1
     )
     late = exchanged(late, PLANE_AXES)
-    small = rounds(small, (("z", 8, 2), ("z", 8, 4), ("x", 4, 1)))
+    small = rounds(small, (("z", 8, 2), ("z", 8, 4), ("x", 4, 1), ("x", 4, 2)))
     from_above = moved(back_down, 1, 0)
     from_left = moved(back_right, 0, 1)
     from_diag = moved(back_diag, 1, 1)
@@ -656,7 +657,7 @@
         0,
     )[None]
     late, small, grad_tokens = lax.optimization_barrier((late, small, grad_tokens))
-    small = rounds(small, (("x", 4, 2), ("yl", 2, 1)))
+    small = rounds(small, (("yl", 2, 1),))
     blocks = pl.pallas_call(
         line_kernel,
         out_shape=shape(8, 24, D, dtype=BF),
@@ -666,28 +667,23 @@
         cost_estimate=cost(2),
         name="line",
     )(early, late, line)
-    sum_hidden, sum_output, sum_qkv, sum_proj = pl.pallas_call(
+    blocks = exchanged(blocks, "z")
+    others = lax.ppermute(small, "yh", [(0, 1), (1, 0)])
+    (
+        sum_hidden, sum_output, sum_qkv, sum_proj,
+        vectors, hidden_total, logit_total, first, second,
+    ) = pl.pallas_call(
         finish_kernel,
-        out_shape=(shape(8 * D), shape(8 * D), shape(8 * 384), shape(8 * 128)),
-        in_specs=whole(1),
-        out_specs=tuple(whole(4)),
+        out_shape=(
+            shape(8 * D), shape(8 * D), shape(8 * 384), shape(8 * 128),
+            shape(8, D), shape(FF), shape(HEADS), shape(3, D), shape(HEADS, D),
+        ),
+        in_specs=whole(3),
+        out_specs=tuple(whole(9)),
         compiler_params=PARAMS,
         cost_estimate=cost(1),
         name="finish",
-    )(exchanged(blocks, "z"))
-    small, sum_hidden, sum_output, sum_qkv, sum_proj = lax.optimization_barrier(
-        (small, sum_hidden, sum_output, sum_qkv, sum_proj)
-    )
-    others = lax.ppermute(small, "yh", [(0, 1), (1, 0)])
-    vectors, hidden_total, logit_total, first, second = pl.pallas_call(
-        unpack_kernel,
-        out_shape=(shape(8, D), shape(FF), shape(HEADS), shape(3, D), shape(HEADS, D)),
-        in_specs=whole(2),
-        out_specs=tuple(whole(5)),
-        compiler_params=PARAMS,
-        cost_estimate=cost(1),
-        name="unpack",
-    )(small, others)
+    )(blocks, small, others)
     return (
         grad_tokens,
         sum_qkv,

time: 139 us -> 133 us (0.957); the launches traced: 138 us -> 130 us
  waiting for transfers between devices: 30.6 us -> 19.1 us
  starting transfers between devices: 45.5 us -> 51.9 us
  Pallas kernels: 49.8 us -> 46.9 us
    ppermute x6, starting transfers between devices: 9.01 us -> 13.8 us  [rounds(): lax.ppermute(small, axis, [(i, i ^ step) for i in range(size)])]
    ppermute x6, waiting for transfers between devices: 14.9 us -> 10.8 us  [rounds(): lax.ppermute(small, axis, [(i, i ^ step) for i in range(size)])]
    all_to_all x3, waiting for transfers between devices: 3.74 us -> 0.01 us  [exchanged(): return lax.all_to_all(blocks, axes, 0, 0)]
    ppermute x1, starting transfers between devices: 0.93 us -> 3.16 us  [local(): others = lax.ppermute(small, 'yh', [(0, 1), (1, 0)])]
    ppermute x1, waiting for transfers between devices: 4.84 us -> 2.69 us  [local(): others = lax.ppermute(small, 'yh', [(0, 1), (1, 0)])]
    ppermute x6, waiting for transfers between devices: 4.32 us -> 2.73 us  [moved(): return lax.ppermute(block, ALL, route)]
    all_to_all x3, starting transfers between devices: 21.4 us -> 19.9 us  [exchanged(): return lax.all_to_all(blocks, axes, 0, 0)]
    pallas_call x1 -> x0, Pallas kernels: 1.51 us -> none  [local(): pl.pallas_call(unpack_kernel, out_shape=(shape(8, D), shape(FF), shape(HE...]
  transfers between devices with their start and end apart: 20 -> 20, of which waited for: 11 -> 9; matrix products, arithmetic and copies ran while one was open for 1% -> 1% of each run, Pallas kernels for 19% -> 20%
where the time goes in v1:
time: 133 us; the launch traced here: 130 us
  starting transfers between devices  51.9 us (39%)
  Pallas kernels  46.9 us (35%)
  waiting for transfers between devices  19.1 us (14%)
  other arithmetic  7.45 us (6%)
  local copies, waits for them, and re-layouts  4.1 us (3%)
    all_to_all x3, starting transfers between devices, exchanged(): return lax.all_to_all(blocks, axes, 0, 0)  19.9 us
    pallas_call x1, Pallas kernels, local(): pl.pallas_call(forward_kernel, out_shape=(shape(D, T, dtype=BF), shape(HE...  17 us
    ppermute x6, starting transfers between devices, rounds(): lax.ppermute(small, axis, [(i, i ^ step) for i in range(size)])  13.8 us
    ppermute x6, starting transfers between devices, moved(): return lax.ppermute(block, ALL, route)  11.7 us
    ppermute x6, waiting for transfers between devices, rounds(): lax.ppermute(small, axis, [(i, i ^ step) for i in range(size)])  10.8 us
    pallas_call x1, Pallas kernels, local(): pl.pallas_call(heads_kernel, out_shape=(shape(T, 3 * D, dtype=BF), shape(...  9.3 us
    pallas_call x1, Pallas kernels, local(): pl.pallas_call(grads_kernel, out_shape=(shape(FF // 2, D, dtype=BF), shap...  3.87 us
    pallas_call x1, Pallas kernels, local(): pl.pallas_call(table_kernel, out_shape=shape(128, 128), in_specs=whole(9)...  3.65 us
  transfers between devices with their start and end apart: 20, of which 9 were waited for; matrix products, arithmetic and copies ran while one was open for 1% of the time, Pallas kernels for 20%

profile of v1, /device:TPU:32, one launch (start us, length us, event | category | flops | bytes accessed | tf_op | source)
XLA Modules:
  0.0 130.3 jit_solution(11134633352038756292)
XLA Ops:
  0.6 1.0 fusion
  1.7 2.8 %collective-permute-start = (bf16[2,8,8,512]{3,2,1,0:T(8,128)(2,1)S(1)}, bf16[2,8,8,512]{3,2,1,0:T(8,128)(2,1)S(1)}, u32[]{:S(2)}, u32[]{:S(2)}) collective-permute-start(bf16[2,8,8,512]{3,2,1,0:T(8,128)(2,1)S(1)} %pad_maximum_fusion.2), channel_id=1, source_target_pairs={{0,240},{1,241},{2,242},{3,243},{4,244},{5,245},{6,246},{7,247},{8... | collective-permute-start | bytes 393224 | tf_op jit(solution)/shard_map/ppermute | solution.py:484
  4.5 2.1 %collective-permute-start.1 = (bf16[2,8,8,512]{3,2,1,0:T(8,128)(2,1)S(1)}, bf16[2,8,8,512]{3,2,1,0:T(8,128)(2,1)S(1)}, u32[]{:S(2)}, u32[]{:S(2)}) collective-permute-start(bf16[2,8,8,512]{3,2,1,0:T(8,128)(2,1)S(1)} %pad_maximum_fusion.3), channel_id=1, source_target_pairs={{0,15},{1,0},{2,1},{3,2},{4,3},{5,4},{6,5},{7,6},{8,7},{9,8},{10,9... | collective-permute-start | bytes 393224 | tf_op jit(solution)/shard_map/ppermute | solution.py:484
  6.7 1.4 %collective-permute-start.2 = (bf16[2,8,8,512]{3,2,1,0:T(8,128)(2,1)S(1)}, bf16[2,8,8,512]{3,2,1,0:T(8,128)(2,1)S(1)}, u32[]{:S(2)}, u32[]{:S(2)}) collective-permute-start(bf16[2,8,8,512]{3,2,1,0:T(8,128)(2,1)S(1)} %pad_maximum_fusion.4), channel_id=1, source_target_pairs={{0,255},{1,240},{2,241},{3,242},{4,243},{5,244},{6,245},{7,246},{8... | collective-permute-start | bytes 393224 | tf_op jit(solution)/shard_map/ppermute | solution.py:484
  8.1 2.8 %bias.1 = (f32[16,16,512]{2,1,0:T(8,128)}, f32[16,1024]{1,0:T(8,128)}) custom-call(f32[2,512]{1,0:T(2,128)} %entry_ref.3, f32[1,512]{1,0:T(1,128)} %bitcast.34, f32[16,512]{1,0:T(8,128)} %bitcast.25), custom_call_target="tpu_custom_call" | custom-call | flops 2500000000 | bytes 10000000 | tf_op jit(solution)/shard_map/bias/pallas_call | solution.py:528
  10.9 2.7 %collective-permute-done.2.diag_ref = bf16[2,8,8,512]{3,2,1,0:T(8,128)(2,1)S(1)} collective-permute-done((bf16[2,8,8,512]{3,2,1,0:T(8,128)(2,1)S(1)}, bf16[2,8,8,512]{3,2,1,0:T(8,128)(2,1)S(1)}, u32[]{:S(2)}, u32[]{:S(2)}) %collective-permute-start.2) | collective-permute-done | bytes 131104 | tf_op jit(solution)/shard_map/ppermute | solution.py:484
  13.6 0.6 copy-done.9
  14.2 17.0 %forward.1 = (bf16[512,256]{1,0:T(8,128)(2,1)}, f32[16,256,256]{2,1,0:T(8,128)}, f32[512,256]{1,0:T(8,128)}, f32[512,256]{1,0:T(8,128)}, f32[2,16,1,256]{3,2,1,0...) custom-call(bf16[1,16,16,512]{3,2,1,0:T(8,128)(2,1)} %tokens_ref.1, ...), custom_call_target="tpu_custom_call" | custom-call | flops 8499999744 | bytes 34000000 | tf_op jit(solution)/shard_map/forward/pallas_call | solution.py:545
  31.3 3.4 %middle.1 = (bf16[512,256]{1,0:T(8,128)(2,1)}, f32[2048,128]{1,0:T(8,128)}, f32[3,512]{1,0:T(4,128)}) custom-call(bf16[512,256]{1,0:T(8,128)(2,1)} %get-tuple-element.76.att_ref, f32[256,512]{1,0:T(8,128)} %get-tuple-element.77.normed_ref, f32[256,1]{1,0:T(8,128)} %get-tuple-element.78.ainverse_ref, f32[256,512]{1,0:T(8,128)} %get-tuple-element.79.gmiddle_ref, ...), custom_call_target="tpu_custom_call" | custom-call | flops 250000000 | bytes 1000000 | tf_op jit(solution)/shard_map/middle/pallas_call | solution.py:572
  34.7 1.0 collective-permute-done.3
  35.7 1.2 add_convert_fusion.2
  36.9 0.3 add_convert_fusion.1
  37.2 1.3 %pad_maximum_fusion = bf16[16,96,512]{2,1,0:T(8,128)(2,1)} fusion(bf16[16,32,512]{2,1,0:T(8,128)(2,1)S(1)} %bitcast.21, bf16[16,64,512]{2,1,0:T(8,128)(2,1)S(1)} %bitcast.19), kind=kLoop, calls=%fused_computation.3 | loop fusion | flops 3145728 | bytes 3145728 | tf_op jit(solution)/shard_map/concatenate | solution.py:581
  38.6 7.1 %all-to-all-start = ((bf16[16,96,512]{2,1,0:T(8,128)(2,1)}), bf16[16,96,512]{2,1,0:T(8,128)(2,1)S(1)}, u32[]{:S(2)}, u32[]{:S(2)}) async-start(bf16[16,96,512]{2,1,0:T(8,128)(2,1)} %pad_maximum_fusion), calls=%async_computation | async-start | bytes 3145728 | tf_op jit(solution)/shard_map/all_to_all | solution.py:496
  45.7 2.7 %collective-permute-start.4 = (bf16[256,512]{1,0:T(8,128)(2,1)S(1)}, bf16[256,512]{1,0:T(8,128)(2,1)S(1)}, u32[]{:S(2)}, u32[]{:S(2)}) collective-permute-start(bf16[256,512]{1,0:T(8,128)(2,1)S(1)} %get-tuple-element.83), channel_id=1, source_target_pairs={{0,32},{32,0},{64,96},{96,64},{128,160},{160,128},{192,224},{224,1... | collective-permute-start | bytes 786440 | tf_op jit(solution)/shard_map/ppermute | solution.py:506
  48.5 9.3 %heads.1 = (bf16[256,1536]{1,0:T(8,128)(2,1)}, f32[3,512]{1,0:T(4,128)}, f32[16,16,512]{2,1,0:T(8,128)}) custom-call(f32[16,256,256]{2,1,0:T(8,128)} %get-tuple-element.69.probs_ref, f32[512,256]{1,0:T(8,128)} %get-tuple-element.70.qunit_ref, f32[512,256]{1,0:T(8,128)} %get-tuple-element.71.kunit_ref, f32[2,16,1,256]{3,2,1,0:T(1,128)} %get-tuple-element.72.inverse_ref, ...), custom_call_target="tpu_custom_call" | custom-call | flops 250000000 | bytes 1000000 | tf_op jit(solution)/shard_map/heads/pallas_call | solution.py:593
  57.8 3.7 %table.1 = f32[128,128]{1,0:T(8,128)} custom-call(f32[2,512]{1,0:T(2,128)} %entry_ref.3, f32[1,512]{1,0:T(1,128)} %bitcast.35, f32[16,512]{1,0:T(8,128)} %bitcast.26, f32[16,1024]{1,0:T(8,128)} %get-tuple-element.84.squashed_ref, f32[16,16,512]{2,1,0:T(8,128)} %get-tuple-element.85.wide_s, f32[3,512]{1,0:T(4,128)} %get-tuple-element.86.sums_ref, ...), custom_call_target="tpu_custom_call" | custom-call | flops 250000000 | bytes 1000000 | tf_op jit(solution)/shard_map/table/pallas_call | solution.py:603
  61.4 3.9 %grads.1 = (bf16[1024,512]{1,0:T(8,128)(2,1)}, bf16[1024,512]{1,0:T(8,128)(2,1)}) custom-call(bf16[512,256]{1,0:T(8,128)(2,1)} %get-tuple-element.68.x_ref, bf16[256,1536]{1,0:T(8,128)(2,1)} %get-tuple-element.97.mixed_ref, f32[2048,128]{1,0:T(8,128)} %get-tuple-element.91.gproj_ref, s32[1]{0:T(128)} %bitcast.10.core_ref), custom_call_target="tpu_custom_call" | custom-call | flops 250000000 | bytes 1000000 | tf_op jit(solution)/shard_map/grads/pallas_call | solution.py:617
  65.3 0.5 collective-permute-start.6
  65.9 1.8 %collective-permute-done.6 = f32[128,128]{1,0:T(8,128)S(1)} collective-permute-done((f32[128,128]{1,0:T(8,128)S(1)}, f32[128,128]{1,0:T(8,128)S(1)}, u32[]{:S(2)}, u32[]{:S(2)}) %collective-permute-start.6) | collective-permute-done | bytes 65568 | tf_op jit(solution)/shard_map/ppermute | solution.py:488
  67.7 0.4 collective-permute-start.7
  68.1 3.1 %window.1 = (bf16[8,8,512]{2,1,0:T(8,128)(2,1)}, bf16[8,8,512]{2,1,0:T(8,128)(2,1)}, bf16[8,8,512]{2,1,0:T(8,128)(2,1)}, bf16[8,8,512]{2,1,0:T(8,128)(2,1)}) custom-call(bf16[256,1536]{1,0:T(8,128)(2,1)} %get-tuple-element.97.mixed_ref, f32[256,512]{1,0:T(8,128)} %get-tuple-element.79.gmiddle_ref, bf16[512,1536]{1,0:T(8,128)(2,1)} %qkv_ref.3), custom_call_target="tpu_custom_call" | custom-call | flops 1000000000 | bytes 4000000 | tf_op jit(solution)/shard_map/window/pallas_call | solution.py:631
  71.2 1.0 collective-permute-done.7
  72.2 1.5 %add_convert_fusion = bf16[1024,512]{1,0:T(8,128)(2,1)S(1)} fusion(bf16[1024,512]{1,0:T(8,128)(2,1)} %collective-permute-done.5, bf16[1024,512]{1,0:T(8,128)(2,1)S(1)} %copy-done.2), kind=kLoop, calls=%fused_computation.1 | loop fusion | flops 2097152 | bytes 3145728 | tf_op jit(solution)/shard_map/convert_element_type | solution.py:492
  73.7 1.2 pad_maximum_fusion.1
  75.0 7.0 %all-to-all-start.1 = ((bf16[16,80,512]{2,1,0:T(8,128)(2,1)}), bf16[16,80,512]{2,1,0:T(8,128)(2,1)S(1)}, u32[]{:S(2)}, u32[]{:S(2)}) async-start(bf16[16,80,512]{2,1,0:T(8,128)(2,1)} %pad_maximum_fusion.1), calls=%async_computation.1 | async-start | bytes 2621440 | tf_op jit(solution)/shard_map/all_to_all | solution.py:496
  82.0 2.7 %collective-permute-start.8 = (f32[128,128]{1,0:T(8,128)S(1)}, f32[128,128]{1,0:T(8,128)S(1)}, u32[]{:S(2)}, u32[]{:S(2)}) collective-permute-start(f32[128,128]{1,0:T(8,128)S(1)} %add.44), channel_id=1, source_target_pairs={{0,64},{32,96},{64,0},{96,32},{128,192},{160,224},{192,128},{224,1... | collective-permute-start | bytes 196616 | tf_op jit(solution)/shard_map/ppermute | solution.py:501
  84.7 2.6 %collective-permute-done.8 = f32[128,128]{1,0:T(8,128)S(1)} collective-permute-done((f32[128,128]{1,0:T(8,128)S(1)}, f32[128,128]{1,0:T(8,128)S(1)}, u32[]{:S(2)}, u32[]{:S(2)}) %collective-permute-start.8) | collective-permute-done | bytes 65568 | tf_op jit(solution)/shard_map/ppermute | solution.py:501
  87.4 5.0 %collective-permute-start.9 = (f32[128,128]{1,0:T(8,128)S(1)}, f32[128,128]{1,0:T(8,128)S(1)}, u32[]{:S(2)}, u32[]{:S(2)}) collective-permute-start(f32[128,128]{1,0:T(8,128)S(1)} %add.47), channel_id=1, source_target_pairs={{0,128},{32,160},{64,192},{96,224},{128,0},{160,32},{192,64},{224,... | collective-permute-start | bytes 196616 | tf_op jit(solution)/shard_map/ppermute | solution.py:501
  92.4 0.5 collective-permute-start.12
  92.9 2.8 %collective-permute-start.13 = (bf16[8,8,512]{2,1,0:T(8,128)(2,1)S(1)}, bf16[8,8,512]{2,1,0:T(8,128)(2,1)S(1)}, u32[]{:S(2)}, u32[]{:S(2)}) collective-permute-start(bf16[8,8,512]{2,1,0:T(8,128)(2,1)S(1)} %copy-done.11), channel_id=1, source_target_pairs={{0,16},{1,17},{2,18},{3,19},{4,20},{5,21},{6,22},{7,23},{8,24},{9,... | collective-permute-start | bytes 196616 | tf_op jit(solution)/shard_map/ppermute | solution.py:484
  95.7 2.1 %collective-permute-start.14 = (bf16[8,8,512]{2,1,0:T(8,128)(2,1)S(1)}, bf16[8,8,512]{2,1,0:T(8,128)(2,1)S(1)}, u32[]{:S(2)}, u32[]{:S(2)}) collective-permute-start(bf16[8,8,512]{2,1,0:T(8,128)(2,1)S(1)} %copy-done.10), channel_id=1, source_target_pairs={{0,1},{1,2},{2,3},{3,4},{4,5},{5,6},{6,7},{7,8},{8,9},{9,10},{10,1... | collective-permute-start | bytes 196616 | tf_op jit(solution)/shard_map/ppermute | solution.py:484
  97.8 1.6 %collective-permute-start.10 = (f32[128,128]{1,0:T(8,128)S(1)}, f32[128,128]{1,0:T(8,128)S(1)}, u32[]{:S(2)}, u32[]{:S(2)}) collective-permute-start(f32[128,128]{1,0:T(8,128)S(1)} %add.48), channel_id=1, source_target_pairs={{0,2},{2,0},{4,6},{6,4},{1,3},{3,1},{5,7},{7,5},{8,10},{10,8},{12,... | collective-permute-start | bytes 196616 | tf_op jit(solution)/shard_map/ppermute | solution.py:501
  99.4 0.9 convert_reduce_fusion.early_ref
  100.3 1.9 %collective-permute-done.10 = f32[128,128]{1,0:T(8,128)S(1)} collective-permute-done((f32[128,128]{1,0:T(8,128)S(1)}, f32[128,128]{1,0:T(8,128)S(1)}, u32[]{:S(2)}, u32[]{:S(2)}) %collective-permute-start.10) | collective-permute-done | bytes 65568 | tf_op jit(solution)/shard_map/ppermute | solution.py:501
  102.2 2.8 %collective-permute-start.11 = (f32[128,128]{1,0:T(8,128)S(1)}, f32[128,128]{1,0:T(8,128)S(1)}, u32[]{:S(2)}, u32[]{:S(2)}) collective-permute-start(f32[128,128]{1,0:T(8,128)S(1)} %add.49), channel_id=1, source_target_pairs={{0,4},{2,6},{4,0},{6,2},{1,5},{3,7},{5,1},{7,3},{8,12},{10,14},{12... | collective-permute-start | bytes 196616 | tf_op jit(solution)/shard_map/ppermute | solution.py:501
  105.0 0.7 maximum_bitcast_fusion
  105.7 2.3 %collective-permute-done.11 = f32[128,128]{1,0:T(8,128)S(1)} collective-permute-done((f32[128,128]{1,0:T(8,128)S(1)}, f32[128,128]{1,0:T(8,128)S(1)}, u32[]{:S(2)}, u32[]{:S(2)}) %collective-permute-start.11) | collective-permute-done | bytes 65568 | tf_op jit(solution)/shard_map/ppermute | solution.py:501
  108.1 1.1 copy-done.1
  109.2 2.3 %line.1 = bf16[8,24,512]{2,1,0:T(8,128)(2,1)} custom-call(f32[96,512]{1,0:T(8,128)} %convert_reduce_fusion.early_ref, bf16[16,80,512]{2,1,0:T(8,128)(2,1)} %copy-done.1, s32[1]{0:T(128)} %bitcast.11.line_ref), custom_call_target="tpu_custom_call" | custom-call | flops 1000000000 | bytes 4000000 | tf_op jit(solution)/shard_map/line/pallas_call | solution.py:661
  111.5 5.8 %all-to-all-start.2 = ((bf16[8,24,512]{2,1,0:T(8,128)(2,1)}), bf16[8,24,512]{2,1,0:T(8,128)(2,1)S(1)}, u32[]{:S(2)}, u32[]{:S(2)}) async-start(bf16[8,24,512]{2,1,0:T(8,128)(2,1)} %line.1), calls=%async_computation.2 | async-start | bytes 393216 | tf_op jit(solution)/shard_map/all_to_all | solution.py:496
  117.2 1.2 collective-permute-start.15
  118.5 3.0 %collective-permute-done.15 = f32[128,128]{1,0:T(8,128)S(1)} collective-permute-done((f32[128,128]{1,0:T(8,128)S(1)}, f32[128,128]{1,0:T(8,128)S(1)}, u32[]{:S(2)}, u32[]{:S(2)}) %collective-permute-start.15) | collective-permute-done | bytes 65568 | tf_op jit(solution)/shard_map/ppermute | solution.py:501
  121.5 3.2 %collective-permute-start.16 = (f32[128,128]{1,0:T(8,128)S(1)}, f32[128,128]{1,0:T(8,128)S(1)}, u32[]{:S(2)}, u32[]{:S(2)}) collective-permute-start(f32[128,128]{1,0:T(8,128)S(1)} %add.51.small_ref), channel_id=1, source_target_pairs={{0,16},{16,0},{1,17},{17,1},{2,18},{18,2},{3,19},{19,3},{4,20},{20... | collective-permute-start | bytes 196616 | tf_op jit(solution)/shard_map/ppermute | solution.py:671
  124.7 2.7 %collective-permute-done.16.others_ref = f32[128,128]{1,0:T(8,128)S(1)} collective-permute-done((f32[128,128]{1,0:T(8,128)S(1)}, f32[128,128]{1,0:T(8,128)S(1)}, u32[]{:S(2)}, u32[]{:S(2)}) %collective-permute-start.16) | collective-permute-done | bytes 65568 | tf_op jit(solution)/shard_map/ppermute | solution.py:671
  127.4 0.6 copy-done.13
  128.0 0.7 copy-done.3
  128.7 1.6 %finish.1 = (f32[4096]{0:T(1024)}, f32[4096]{0:T(1024)}, f32[3072]{0:T(1024)}, f32[1024]{0:T(1024)}, f32[8,512]{1,0:T(8,128)}, /*index=5*/f32[2048]{0:T(1024)}, ...) custom-call(bf16[8,24,512]{2,1,0:T(8,128)(2,1)} %copy-done.3, f32[128,128]{1,0:T(8,128)} %copy-done.5, f32[128,128]{1,0:T(8,128)} %copy-done.13), custom_call_target="tpu_custom_call" | custom-call | flops 500000000 | bytes 2000000 | tf_op jit(solution)/shard_map/finish/pallas_call | solution.py:675
  (49 shorter events, 0.5 us)
Async XLA Ops:
  1.7 9.2 %collective-permute-start = (bf16[2,8,8,512]{3,2,1,0:T(8,128)(2,1)S(1)}, bf16[2,8,8,512]{3,2,1,0:T(8,128)(2,1)S(1)}, u32[]{:S(2)}, u32[]{:S(2)}) collective-permute-start(bf16[2,8,8,512]{3,2,1,0:T(8,128)(2,1)S(1)} %pad_maximum_fusion.2), channel_id=1, source_target_pairs={{0,240},{1,241},{2,242},{3,243},{4,244},{5,245},{6,246},{7,247},{8... | collective-permute-start | bytes 393224 | tf_op jit(solution)/shard_map/ppermute | solution.py:484
  4.5 6.3 %collective-permute-start.1 = (bf16[2,8,8,512]{3,2,1,0:T(8,128)(2,1)S(1)}, bf16[2,8,8,512]{3,2,1,0:T(8,128)(2,1)S(1)}, u32[]{:S(2)}, u32[]{:S(2)}) collective-permute-start(bf16[2,8,8,512]{3,2,1,0:T(8,128)(2,1)S(1)} %pad_maximum_fusion.3), channel_id=1, source_target_pairs={{0,15},{1,0},{2,1},{3,2},{4,3},{5,4},{6,5},{7,6},{8,7},{9,8},{10,9... | collective-permute-start | bytes 393224 | tf_op jit(solution)/shard_map/ppermute | solution.py:484
  6.7 6.9 %collective-permute-start.2 = (bf16[2,8,8,512]{3,2,1,0:T(8,128)(2,1)S(1)}, bf16[2,8,8,512]{3,2,1,0:T(8,128)(2,1)S(1)}, u32[]{:S(2)}, u32[]{:S(2)}) collective-permute-start(bf16[2,8,8,512]{3,2,1,0:T(8,128)(2,1)S(1)} %pad_maximum_fusion.4), channel_id=1, source_target_pairs={{0,255},{1,240},{2,241},{3,242},{4,243},{5,244},{6,245},{7,246},{8... | collective-permute-start | bytes 393224 | tf_op jit(solution)/shard_map/ppermute | solution.py:484
  10.9 2.7 %copy-start.7 = (bf16[2,8,8,512]{3,2,1,0:T(8,128)(2,1)}, bf16[2,8,8,512]{3,2,1,0:T(8,128)(2,1)S(1)}, u32[]{:S(2)}) copy-start(bf16[2,8,8,512]{3,2,1,0:T(8,128)(2,1)S(1)} %collective-permute-done.down_ref) | copy-start | bytes 393220
  10.9 2.7 %copy-start.8 = (bf16[2,8,8,512]{3,2,1,0:T(8,128)(2,1)}, bf16[2,8,8,512]{3,2,1,0:T(8,128)(2,1)S(1)}, u32[]{:S(2)}) copy-start(bf16[2,8,8,512]{3,2,1,0:T(8,128)(2,1)S(1)} %collective-permute-done.1.right_ref) | copy-start | bytes 393220
  13.6 0.6 copy-start.9
  31.2 5.6 %copy-start = (bf16[2048,512]{1,0:T(8,128)(2,1)S(1)}, bf16[2048,512]{1,0:T(8,128)(2,1)}, u32[]{:S(2)}) copy-start(bf16[2048,512]{1,0:T(8,128)(2,1)} %get-tuple-element.74) | copy-start | bytes 6291460
  31.2 4.5 %collective-permute-start.3 = (bf16[2048,512]{1,0:T(8,128)(2,1)}, bf16[2048,512]{1,0:T(8,128)(2,1)S(1)}, u32[]{:S(2)}, u32[]{:S(2)}) collective-permute-start(bf16[2048,512]{1,0:T(8,128)(2,1)} %get-tuple-element.75), channel_id=1, source_target_pairs={{0,1},{1,0},{2,3},{3,2},{4,5},{5,4},{6,7},{7,6},{8,9},{9,8},{10,11... | collective-permute-start | bytes 6291464 | tf_op jit(solution)/shard_map/ppermute | solution.py:488
  38.6 33.6 %all-to-all-start = ((bf16[16,96,512]{2,1,0:T(8,128)(2,1)}), bf16[16,96,512]{2,1,0:T(8,128)(2,1)S(1)}, u32[]{:S(2)}, u32[]{:S(2)}) async-start(bf16[16,96,512]{2,1,0:T(8,128)(2,1)} %pad_maximum_fusion), calls=%async_computation | async-start | bytes 3145728 | tf_op jit(solution)/shard_map/all_to_all | solution.py:496
  45.7 15.7 %collective-permute-start.4 = (bf16[256,512]{1,0:T(8,128)(2,1)S(1)}, bf16[256,512]{1,0:T(8,128)(2,1)S(1)}, u32[]{:S(2)}, u32[]{:S(2)}) collective-permute-start(bf16[256,512]{1,0:T(8,128)(2,1)S(1)} %get-tuple-element.83), channel_id=1, source_target_pairs={{0,32},{32,0},{64,96},{96,64},{128,160},{160,128},{192,224},{224,1... | collective-permute-start | bytes 786440 | tf_op jit(solution)/shard_map/ppermute | solution.py:506
  61.4 3.9 %copy-start.4 = (f32[128,128]{1,0:T(8,128)S(1)}, f32[128,128]{1,0:T(8,128)}, u32[]{:S(2)}) copy-start(f32[128,128]{1,0:T(8,128)} %table.1) | copy-start | bytes 196612
  65.3 6.9 %collective-permute-start.5 = (bf16[1024,512]{1,0:T(8,128)(2,1)}, bf16[1024,512]{1,0:T(8,128)(2,1)}, u32[]{:S(2)}, u32[]{:S(2)}) collective-permute-start(bf16[1024,512]{1,0:T(8,128)(2,1)} %get-tuple-element.92), channel_id=1, source_target_pairs={{0,1},{1,0},{2,3},{3,2},{4,5},{5,4},{6,7},{7,6},{8,9},{9,8},{10,11... | collective-permute-start | bytes 3145736 | tf_op jit(solution)/shard_map/ppermute | solution.py:488
  65.3 2.4 %collective-permute-start.6 = (f32[128,128]{1,0:T(8,128)S(1)}, f32[128,128]{1,0:T(8,128)S(1)}, u32[]{:S(2)}, u32[]{:S(2)}) collective-permute-start(f32[128,128]{1,0:T(8,128)S(1)} %copy-done.4), channel_id=1, source_target_pairs={{0,1},{1,0},{2,3},{3,2},{4,5},{5,4},{6,7},{7,6},{8,9},{9,8},{10,11... | collective-permute-start | bytes 196616 | tf_op jit(solution)/shard_map/ppermute | solution.py:488
  65.9 6.3 %copy-start.2 = (bf16[1024,512]{1,0:T(8,128)(2,1)S(1)}, bf16[1024,512]{1,0:T(8,128)(2,1)}, u32[]{:S(2)}) copy-start(bf16[1024,512]{1,0:T(8,128)(2,1)} %get-tuple-element.102) | copy-start | bytes 3145732
  67.7 4.5 %collective-permute-start.7 = (f32[128,128]{1,0:T(8,128)S(1)}, f32[128,128]{1,0:T(8,128)S(1)}, u32[]{:S(2)}, u32[]{:S(2)}) collective-permute-start(f32[128,128]{1,0:T(8,128)S(1)} %add.43), channel_id=1, source_target_pairs={{0,32},{32,0},{64,96},{96,64},{128,160},{160,128},{192,224},{224,1... | collective-permute-start | bytes 196616 | tf_op jit(solution)/shard_map/ppermute | solution.py:501
  73.7 18.7 %copy-start.12 = (bf16[8,8,512]{2,1,0:T(8,128)(2,1)S(1)}, bf16[8,8,512]{2,1,0:T(8,128)(2,1)}, u32[]{:S(2)}) copy-start(bf16[8,8,512]{2,1,0:T(8,128)(2,1)} %get-tuple-element.107) | copy-start | bytes 196612
  73.7 19.2 %copy-start.11 = (bf16[8,8,512]{2,1,0:T(8,128)(2,1)S(1)}, bf16[8,8,512]{2,1,0:T(8,128)(2,1)}, u32[]{:S(2)}) copy-start(bf16[8,8,512]{2,1,0:T(8,128)(2,1)} %get-tuple-element.108) | copy-start | bytes 196612
  73.7 22.0 %copy-start.10 = (bf16[8,8,512]{2,1,0:T(8,128)(2,1)S(1)}, bf16[8,8,512]{2,1,0:T(8,128)(2,1)}, u32[]{:S(2)}) copy-start(bf16[8,8,512]{2,1,0:T(8,128)(2,1)} %get-tuple-element.109) | copy-start | bytes 196612
  75.0 30.0 %copy-start.6 = (bf16[8,8,512]{2,1,0:T(8,128)(2,1)S(1)}, bf16[8,8,512]{2,1,0:T(8,128)(2,1)}, u32[]{:S(2)}) copy-start(bf16[8,8,512]{2,1,0:T(8,128)(2,1)} %get-tuple-element.110) | copy-start | bytes 196612
  75.0 33.1 %all-to-all-start.1 = ((bf16[16,80,512]{2,1,0:T(8,128)(2,1)}), bf16[16,80,512]{2,1,0:T(8,128)(2,1)S(1)}, u32[]{:S(2)}, u32[]{:S(2)}) async-start(bf16[16,80,512]{2,1,0:T(8,128)(2,1)} %pad_maximum_fusion.1), calls=%async_computation.1 | async-start | bytes 2621440 | tf_op jit(solution)/shard_map/all_to_all | solution.py:496
  82.0 5.4 %collective-permute-start.8 = (f32[128,128]{1,0:T(8,128)S(1)}, f32[128,128]{1,0:T(8,128)S(1)}, u32[]{:S(2)}, u32[]{:S(2)}) collective-permute-start(f32[128,128]{1,0:T(8,128)S(1)} %add.44), channel_id=1, source_target_pairs={{0,64},{32,96},{64,0},{96,32},{128,192},{160,224},{192,128},{224,1... | collective-permute-start | bytes 196616 | tf_op jit(solution)/shard_map/ppermute | solution.py:501
  87.4 10.5 %collective-permute-start.9 = (f32[128,128]{1,0:T(8,128)S(1)}, f32[128,128]{1,0:T(8,128)S(1)}, u32[]{:S(2)}, u32[]{:S(2)}) collective-permute-start(f32[128,128]{1,0:T(8,128)S(1)} %add.47), channel_id=1, source_target_pairs={{0,128},{32,160},{64,192},{96,224},{128,0},{160,32},{192,64},{224,... | collective-permute-start | bytes 196616 | tf_op jit(solution)/shard_map/ppermute | solution.py:501
  92.4 12.6 %collective-permute-start.12 = (bf16[8,8,512]{2,1,0:T(8,128)(2,1)S(1)}, bf16[8,8,512]{2,1,0:T(8,128)(2,1)S(1)}, u32[]{:S(2)}, u32[]{:S(2)}) collective-permute-start(bf16[8,8,512]{2,1,0:T(8,128)(2,1)S(1)} %copy-done.12), channel_id=1, source_target_pairs={{0,17},{1,18},{2,19},{3,20},{4,21},{5,22},{6,23},{7,24},{8,25},{9,... | collective-permute-start | bytes 196616 | tf_op jit(solution)/shard_map/ppermute | solution.py:484
  92.9 12.0 %collective-permute-start.13 = (bf16[8,8,512]{2,1,0:T(8,128)(2,1)S(1)}, bf16[8,8,512]{2,1,0:T(8,128)(2,1)S(1)}, u32[]{:S(2)}, u32[]{:S(2)}) collective-permute-start(bf16[8,8,512]{2,1,0:T(8,128)(2,1)S(1)} %copy-done.11), channel_id=1, source_target_pairs={{0,16},{1,17},{2,18},{3,19},{4,20},{5,21},{6,22},{7,23},{8,24},{9,... | collective-permute-start | bytes 196616 | tf_op jit(solution)/shard_map/ppermute | solution.py:484
  95.7 9.2 %collective-permute-start.14 = (bf16[8,8,512]{2,1,0:T(8,128)(2,1)S(1)}, bf16[8,8,512]{2,1,0:T(8,128)(2,1)S(1)}, u32[]{:S(2)}, u32[]{:S(2)}) collective-permute-start(bf16[8,8,512]{2,1,0:T(8,128)(2,1)S(1)} %copy-done.10), channel_id=1, source_target_pairs={{0,1},{1,2},{2,3},{3,4},{4,5},{5,6},{6,7},{7,8},{8,9},{9,10},{10,1... | collective-permute-start | bytes 196616 | tf_op jit(solution)/shard_map/ppermute | solution.py:484
  97.8 4.4 %collective-permute-start.10 = (f32[128,128]{1,0:T(8,128)S(1)}, f32[128,128]{1,0:T(8,128)S(1)}, u32[]{:S(2)}, u32[]{:S(2)}) collective-permute-start(f32[128,128]{1,0:T(8,128)S(1)} %add.48), channel_id=1, source_target_pairs={{0,2},{2,0},{4,6},{6,4},{1,3},{3,1},{5,7},{7,5},{8,10},{10,8},{12,... | collective-permute-start | bytes 196616 | tf_op jit(solution)/shard_map/ppermute | solution.py:501
  102.2 5.9 %collective-permute-start.11 = (f32[128,128]{1,0:T(8,128)S(1)}, f32[128,128]{1,0:T(8,128)S(1)}, u32[]{:S(2)}, u32[]{:S(2)}) collective-permute-start(f32[128,128]{1,0:T(8,128)S(1)} %add.49), channel_id=1, source_target_pairs={{0,4},{2,6},{4,0},{6,2},{1,5},{3,7},{5,1},{7,3},{8,12},{10,14},{12... | collective-permute-start | bytes 196616 | tf_op jit(solution)/shard_map/ppermute | solution.py:501
  108.1 1.1 copy-start.1
  111.5 15.9 %all-to-all-start.2 = ((bf16[8,24,512]{2,1,0:T(8,128)(2,1)}), bf16[8,24,512]{2,1,0:T(8,128)(2,1)S(1)}, u32[]{:S(2)}, u32[]{:S(2)}) async-start(bf16[8,24,512]{2,1,0:T(8,128)(2,1)} %line.1), calls=%async_computation.2 | async-start | bytes 393216 | tf_op jit(solution)/shard_map/all_to_all | solution.py:496
  117.2 4.3 %collective-permute-start.15 = (f32[128,128]{1,0:T(8,128)S(1)}, f32[128,128]{1,0:T(8,128)S(1)}, u32[]{:S(2)}, u32[]{:S(2)}) collective-permute-start(f32[128,128]{1,0:T(8,128)S(1)} %add.50), channel_id=1, source_target_pairs={{0,8},{8,0},{1,9},{9,1},{2,10},{10,2},{3,11},{11,3},{4,12},{12,4},... | collective-permute-start | bytes 196616 | tf_op jit(solution)/shard_map/ppermute | solution.py:501
  121.5 5.9 %copy-start.5 = (f32[128,128]{1,0:T(8,128)}, f32[128,128]{1,0:T(8,128)S(1)}, u32[]{:S(2)}) copy-start(f32[128,128]{1,0:T(8,128)S(1)} %add.51.small_ref) | copy-start | bytes 196612
  121.5 5.9 %collective-permute-start.16 = (f32[128,128]{1,0:T(8,128)S(1)}, f32[128,128]{1,0:T(8,128)S(1)}, u32[]{:S(2)}, u32[]{:S(2)}) collective-permute-start(f32[128,128]{1,0:T(8,128)S(1)} %add.51.small_ref), channel_id=1, source_target_pairs={{0,16},{16,0},{1,17},{17,1},{2,18},{18,2},{3,19},{19,3},{4,20},{20... | collective-permute-start | bytes 196616 | tf_op jit(solution)/shard_map/ppermute | solution.py:671
  127.4 0.6 copy-start.13
  128.0 0.7 copy-start.3

commit v2 on v1

--- a/solution.py
+++ b/solution.py
@@ -273,7 +273,7 @@
         att_s[at, :] = dot(value_s[at, :], probs.astype(BF), 1, 0).astype(BF)
         return carry
 
-    lax.fori_loop(0, HEADS, head, 0, unroll=4)
+    lax.fori_loop(0, HEADS, head, 0, unroll=8)
 
     store(att_s, att_ref)
     projected = dot(att_s[...], proj_ref[...], 0, 0) + pbias_ref[...]
@@ -408,7 +408,7 @@
         wide_s[h] = wide
         return carry
 
-    logits = lax.fori_loop(0, HEADS, head, jnp.zeros((1, T), F4), unroll=4)
+    logits = lax.fori_loop(0, HEADS, head, jnp.zeros((1, T), F4), unroll=8)
     sums_ref[2:3, :] = jnp.concatenate([logits, jnp.zeros((1, D - T), F4)], 1)
 
     ones = jnp.ones((8, T), F4)

time: 133 us -> 132 us (level)
  no operation moved by 1% of the time
where the time goes in v2:
time: 132 us; the launch traced here: 130 us
  starting transfers between devices  52.1 us (39%)
  Pallas kernels  46.2 us (35%)
  waiting for transfers between devices  19 us (14%)
  other arithmetic  7.45 us (6%)
  local copies, waits for them, and re-layouts  4.1 us (3%)
    all_to_all x3, starting transfers between devices, exchanged(): return lax.all_to_all(blocks, axes, 0, 0)  20 us
    pallas_call x1, Pallas kernels, local(): pl.pallas_call(forward_kernel, out_shape=(shape(D, T, dtype=BF), shape(HE...  16.7 us
    ppermute x6, starting transfers between devices, rounds(): lax.ppermute(small, axis, [(i, i ^ step) for i in range(size)])  13.7 us
    ppermute x6, starting transfers between devices, moved(): return lax.ppermute(block, ALL, route)  11.8 us
    ppermute x6, waiting for transfers between devices, rounds(): lax.ppermute(small, axis, [(i, i ^ step) for i in range(size)])  10.8 us
    pallas_call x1, Pallas kernels, local(): pl.pallas_call(heads_kernel, out_shape=(shape(T, 3 * D, dtype=BF), shape(...  8.84 us
    pallas_call x1, Pallas kernels, local(): pl.pallas_call(grads_kernel, out_shape=(shape(FF // 2, D, dtype=BF), shap...  3.87 us
    pallas_call x1, Pallas kernels, local(): pl.pallas_call(table_kernel, out_shape=shape(128, 128), in_specs=whole(9)...  3.65 us
  transfers between devices with their start and end apart: 20, of which 9 were waited for; matrix products, arithmetic and copies ran while one was open for 1% of the time, Pallas kernels for 20%

profile of v2, /device:TPU:32, one launch (start us, length us, event | category | flops | bytes accessed | tf_op | source)
XLA Modules:
  0.0 129.6 jit_solution(13302228121089840869)
XLA Ops:
  0.6 1.0 fusion
  1.7 2.8 %collective-permute-start = (bf16[2,8,8,512]{3,2,1,0:T(8,128)(2,1)S(1)}, bf16[2,8,8,512]{3,2,1,0:T(8,128)(2,1)S(1)}, u32[]{:S(2)}, u32[]{:S(2)}) collective-permute-start(bf16[2,8,8,512]{3,2,1,0:T(8,128)(2,1)S(1)} %pad_maximum_fusion.2), channel_id=1, source_target_pairs={{0,240},{1,241},{2,242},{3,243},{4,244},{5,245},{6,246},{7,247},{8... | collective-permute-start | bytes 393224 | tf_op jit(solution)/shard_map/ppermute | solution.py:484
  4.5 2.1 %collective-permute-start.1 = (bf16[2,8,8,512]{3,2,1,0:T(8,128)(2,1)S(1)}, bf16[2,8,8,512]{3,2,1,0:T(8,128)(2,1)S(1)}, u32[]{:S(2)}, u32[]{:S(2)}) collective-permute-start(bf16[2,8,8,512]{3,2,1,0:T(8,128)(2,1)S(1)} %pad_maximum_fusion.3), channel_id=1, source_target_pairs={{0,15},{1,0},{2,1},{3,2},{4,3},{5,4},{6,5},{7,6},{8,7},{9,8},{10,9... | collective-permute-start | bytes 393224 | tf_op jit(solution)/shard_map/ppermute | solution.py:484
  6.7 1.4 %collective-permute-start.2 = (bf16[2,8,8,512]{3,2,1,0:T(8,128)(2,1)S(1)}, bf16[2,8,8,512]{3,2,1,0:T(8,128)(2,1)S(1)}, u32[]{:S(2)}, u32[]{:S(2)}) collective-permute-start(bf16[2,8,8,512]{3,2,1,0:T(8,128)(2,1)S(1)} %pad_maximum_fusion.4), channel_id=1, source_target_pairs={{0,255},{1,240},{2,241},{3,242},{4,243},{5,244},{6,245},{7,246},{8... | collective-permute-start | bytes 393224 | tf_op jit(solution)/shard_map/ppermute | solution.py:484
  8.1 2.8 %bias.1 = (f32[16,16,512]{2,1,0:T(8,128)}, f32[16,1024]{1,0:T(8,128)}) custom-call(f32[2,512]{1,0:T(2,128)} %entry_ref.3, f32[1,512]{1,0:T(1,128)} %bitcast.34, f32[16,512]{1,0:T(8,128)} %bitcast.25), custom_call_target="tpu_custom_call" | custom-call | flops 2500000000 | bytes 10000000 | tf_op jit(solution)/shard_map/bias/pallas_call | solution.py:528
  10.9 2.7 %collective-permute-done.2.diag_ref = bf16[2,8,8,512]{3,2,1,0:T(8,128)(2,1)S(1)} collective-permute-done((bf16[2,8,8,512]{3,2,1,0:T(8,128)(2,1)S(1)}, bf16[2,8,8,512]{3,2,1,0:T(8,128)(2,1)S(1)}, u32[]{:S(2)}, u32[]{:S(2)}) %collective-permute-start.2) | collective-permute-done | bytes 131104 | tf_op jit(solution)/shard_map/ppermute | solution.py:484
  13.6 0.6 copy-done.9
  14.2 16.7 %forward.1 = (bf16[512,256]{1,0:T(8,128)(2,1)}, f32[16,256,256]{2,1,0:T(8,128)}, f32[512,256]{1,0:T(8,128)}, f32[512,256]{1,0:T(8,128)}, f32[2,16,1,256]{3,2,1,0...) custom-call(bf16[1,16,16,512]{3,2,1,0:T(8,128)(2,1)} %tokens_ref.1, ...), custom_call_target="tpu_custom_call" | custom-call | flops 8499999744 | bytes 34000000 | tf_op jit(solution)/shard_map/forward/pallas_call | solution.py:545
  31.2 3.4 %middle.1 = (bf16[512,256]{1,0:T(8,128)(2,1)}, f32[2048,128]{1,0:T(8,128)}, f32[3,512]{1,0:T(4,128)}) custom-call(bf16[512,256]{1,0:T(8,128)(2,1)} %get-tuple-element.76.att_ref, f32[256,512]{1,0:T(8,128)} %get-tuple-element.77.normed_ref, f32[256,1]{1,0:T(8,128)} %get-tuple-element.78.ainverse_ref, f32[256,512]{1,0:T(8,128)} %get-tuple-element.79.gmiddle_ref, ...), custom_call_target="tpu_custom_call" | custom-call | flops 250000000 | bytes 1000000 | tf_op jit(solution)/shard_map/middle/pallas_call | solution.py:572
  34.6 1.0 collective-permute-done.3
  35.5 1.2 add_convert_fusion.2
  36.7 0.3 add_convert_fusion.1
  37.0 1.3 %pad_maximum_fusion = bf16[16,96,512]{2,1,0:T(8,128)(2,1)} fusion(bf16[16,32,512]{2,1,0:T(8,128)(2,1)S(1)} %bitcast.21, bf16[16,64,512]{2,1,0:T(8,128)(2,1)S(1)} %bitcast.19), kind=kLoop, calls=%fused_computation.3 | loop fusion | flops 3145728 | bytes 3145728 | tf_op jit(solution)/shard_map/concatenate | solution.py:581
  38.5 7.1 %all-to-all-start = ((bf16[16,96,512]{2,1,0:T(8,128)(2,1)}), bf16[16,96,512]{2,1,0:T(8,128)(2,1)S(1)}, u32[]{:S(2)}, u32[]{:S(2)}) async-start(bf16[16,96,512]{2,1,0:T(8,128)(2,1)} %pad_maximum_fusion), calls=%async_computation | async-start | bytes 3145728 | tf_op jit(solution)/shard_map/all_to_all | solution.py:496
  45.6 2.5 %collective-permute-start.4 = (bf16[256,512]{1,0:T(8,128)(2,1)S(1)}, bf16[256,512]{1,0:T(8,128)(2,1)S(1)}, u32[]{:S(2)}, u32[]{:S(2)}) collective-permute-start(bf16[256,512]{1,0:T(8,128)(2,1)S(1)} %get-tuple-element.83), channel_id=1, source_target_pairs={{0,32},{32,0},{64,96},{96,64},{128,160},{160,128},{192,224},{224,1... | collective-permute-start | bytes 786440 | tf_op jit(solution)/shard_map/ppermute | solution.py:506
  48.1 8.8 %heads.1 = (bf16[256,1536]{1,0:T(8,128)(2,1)}, f32[3,512]{1,0:T(4,128)}, f32[16,16,512]{2,1,0:T(8,128)}) custom-call(f32[16,256,256]{2,1,0:T(8,128)} %get-tuple-element.69.probs_ref, f32[512,256]{1,0:T(8,128)} %get-tuple-element.70.qunit_ref, f32[512,256]{1,0:T(8,128)} %get-tuple-element.71.kunit_ref, f32[2,16,1,256]{3,2,1,0:T(1,128)} %get-tuple-element.72.inverse_ref, ...), custom_call_target="tpu_custom_call" | custom-call | flops 250000000 | bytes 1000000 | tf_op jit(solution)/shard_map/heads/pallas_call | solution.py:593
  57.0 3.6 %table.1 = f32[128,128]{1,0:T(8,128)} custom-call(f32[2,512]{1,0:T(2,128)} %entry_ref.3, f32[1,512]{1,0:T(1,128)} %bitcast.35, f32[16,512]{1,0:T(8,128)} %bitcast.26, f32[16,1024]{1,0:T(8,128)} %get-tuple-element.84.squashed_ref, f32[16,16,512]{2,1,0:T(8,128)} %get-tuple-element.85.wide_s, f32[3,512]{1,0:T(4,128)} %get-tuple-element.86.sums_ref, ...), custom_call_target="tpu_custom_call" | custom-call | flops 250000000 | bytes 1000000 | tf_op jit(solution)/shard_map/table/pallas_call | solution.py:603
  60.6 3.9 %grads.1 = (bf16[1024,512]{1,0:T(8,128)(2,1)}, bf16[1024,512]{1,0:T(8,128)(2,1)}) custom-call(bf16[512,256]{1,0:T(8,128)(2,1)} %get-tuple-element.68.x_ref, bf16[256,1536]{1,0:T(8,128)(2,1)} %get-tuple-element.97.mixed_ref, f32[2048,128]{1,0:T(8,128)} %get-tuple-element.91.gproj_ref, s32[1]{0:T(128)} %bitcast.10.core_ref), custom_call_target="tpu_custom_call" | custom-call | flops 250000000 | bytes 1000000 | tf_op jit(solution)/shard_map/grads/pallas_call | solution.py:617
  64.5 0.5 collective-permute-start.6
  65.1 1.8 %collective-permute-done.6 = f32[128,128]{1,0:T(8,128)S(1)} collective-permute-done((f32[128,128]{1,0:T(8,128)S(1)}, f32[128,128]{1,0:T(8,128)S(1)}, u32[]{:S(2)}, u32[]{:S(2)}) %collective-permute-start.6) | collective-permute-done | bytes 65568 | tf_op jit(solution)/shard_map/ppermute | solution.py:488
  66.9 0.4 collective-permute-start.7
  67.3 3.1 %window.1 = (bf16[8,8,512]{2,1,0:T(8,128)(2,1)}, bf16[8,8,512]{2,1,0:T(8,128)(2,1)}, bf16[8,8,512]{2,1,0:T(8,128)(2,1)}, bf16[8,8,512]{2,1,0:T(8,128)(2,1)}) custom-call(bf16[256,1536]{1,0:T(8,128)(2,1)} %get-tuple-element.97.mixed_ref, f32[256,512]{1,0:T(8,128)} %get-tuple-element.79.gmiddle_ref, bf16[512,1536]{1,0:T(8,128)(2,1)} %qkv_ref.3), custom_call_target="tpu_custom_call" | custom-call | flops 1000000000 | bytes 4000000 | tf_op jit(solution)/shard_map/window/pallas_call | solution.py:631
  70.4 0.9 collective-permute-done.7
  71.4 1.5 %add_convert_fusion = bf16[1024,512]{1,0:T(8,128)(2,1)S(1)} fusion(bf16[1024,512]{1,0:T(8,128)(2,1)} %collective-permute-done.5, bf16[1024,512]{1,0:T(8,128)(2,1)S(1)} %copy-done.2), kind=kLoop, calls=%fused_computation.1 | loop fusion | flops 2097152 | bytes 3145728 | tf_op jit(solution)/shard_map/convert_element_type | solution.py:492
  72.9 1.2 pad_maximum_fusion.1
  74.2 7.2 %all-to-all-start.1 = ((bf16[16,80,512]{2,1,0:T(8,128)(2,1)}), bf16[16,80,512]{2,1,0:T(8,128)(2,1)S(1)}, u32[]{:S(2)}, u32[]{:S(2)}) async-start(bf16[16,80,512]{2,1,0:T(8,128)(2,1)} %pad_maximum_fusion.1), calls=%async_computation.1 | async-start | bytes 2621440 | tf_op jit(solution)/shard_map/all_to_all | solution.py:496
  81.4 2.7 %collective-permute-start.8 = (f32[128,128]{1,0:T(8,128)S(1)}, f32[128,128]{1,0:T(8,128)S(1)}, u32[]{:S(2)}, u32[]{:S(2)}) collective-permute-start(f32[128,128]{1,0:T(8,128)S(1)} %add.44), channel_id=1, source_target_pairs={{0,64},{32,96},{64,0},{96,32},{128,192},{160,224},{192,128},{224,1... | collective-permute-start | bytes 196616 | tf_op jit(solution)/shard_map/ppermute | solution.py:501
  84.1 2.6 %collective-permute-done.8 = f32[128,128]{1,0:T(8,128)S(1)} collective-permute-done((f32[128,128]{1,0:T(8,128)S(1)}, f32[128,128]{1,0:T(8,128)S(1)}, u32[]{:S(2)}, u32[]{:S(2)}) %collective-permute-start.8) | collective-permute-done | bytes 65568 | tf_op jit(solution)/shard_map/ppermute | solution.py:501
  86.7 5.0 %collective-permute-start.9 = (f32[128,128]{1,0:T(8,128)S(1)}, f32[128,128]{1,0:T(8,128)S(1)}, u32[]{:S(2)}, u32[]{:S(2)}) collective-permute-start(f32[128,128]{1,0:T(8,128)S(1)} %add.47), channel_id=1, source_target_pairs={{0,128},{32,160},{64,192},{96,224},{128,0},{160,32},{192,64},{224,... | collective-permute-start | bytes 196616 | tf_op jit(solution)/shard_map/ppermute | solution.py:501
  91.7 0.5 collective-permute-start.12
  92.3 3.0 %collective-permute-start.13 = (bf16[8,8,512]{2,1,0:T(8,128)(2,1)S(1)}, bf16[8,8,512]{2,1,0:T(8,128)(2,1)S(1)}, u32[]{:S(2)}, u32[]{:S(2)}) collective-permute-start(bf16[8,8,512]{2,1,0:T(8,128)(2,1)S(1)} %copy-done.11), channel_id=1, source_target_pairs={{0,16},{1,17},{2,18},{3,19},{4,20},{5,21},{6,22},{7,23},{8,24},{9,... | collective-permute-start | bytes 196616 | tf_op jit(solution)/shard_map/ppermute | solution.py:484
  95.3 1.9 %collective-permute-start.14 = (bf16[8,8,512]{2,1,0:T(8,128)(2,1)S(1)}, bf16[8,8,512]{2,1,0:T(8,128)(2,1)S(1)}, u32[]{:S(2)}, u32[]{:S(2)}) collective-permute-start(bf16[8,8,512]{2,1,0:T(8,128)(2,1)S(1)} %copy-done.10), channel_id=1, source_target_pairs={{0,1},{1,2},{2,3},{3,4},{4,5},{5,6},{6,7},{7,8},{8,9},{9,10},{10,1... | collective-permute-start | bytes 196616 | tf_op jit(solution)/shard_map/ppermute | solution.py:484
  97.2 1.6 %collective-permute-start.10 = (f32[128,128]{1,0:T(8,128)S(1)}, f32[128,128]{1,0:T(8,128)S(1)}, u32[]{:S(2)}, u32[]{:S(2)}) collective-permute-start(f32[128,128]{1,0:T(8,128)S(1)} %add.48), channel_id=1, source_target_pairs={{0,2},{2,0},{4,6},{6,4},{1,3},{3,1},{5,7},{7,5},{8,10},{10,8},{12,... | collective-permute-start | bytes 196616 | tf_op jit(solution)/shard_map/ppermute | solution.py:501
  98.7 0.9 convert_reduce_fusion.early_ref
  99.6 1.9 %collective-permute-done.10 = f32[128,128]{1,0:T(8,128)S(1)} collective-permute-done((f32[128,128]{1,0:T(8,128)S(1)}, f32[128,128]{1,0:T(8,128)S(1)}, u32[]{:S(2)}, u32[]{:S(2)}) %collective-permute-start.10) | collective-permute-done | bytes 65568 | tf_op jit(solution)/shard_map/ppermute | solution.py:501
  101.5 2.8 %collective-permute-start.11 = (f32[128,128]{1,0:T(8,128)S(1)}, f32[128,128]{1,0:T(8,128)S(1)}, u32[]{:S(2)}, u32[]{:S(2)}) collective-permute-start(f32[128,128]{1,0:T(8,128)S(1)} %add.49), channel_id=1, source_target_pairs={{0,4},{2,6},{4,0},{6,2},{1,5},{3,7},{5,1},{7,3},{8,12},{10,14},{12... | collective-permute-start | bytes 196616 | tf_op jit(solution)/shard_map/ppermute | solution.py:501
  104.3 0.7 maximum_bitcast_fusion
  105.1 2.3 %collective-permute-done.11 = f32[128,128]{1,0:T(8,128)S(1)} collective-permute-done((f32[128,128]{1,0:T(8,128)S(1)}, f32[128,128]{1,0:T(8,128)S(1)}, u32[]{:S(2)}, u32[]{:S(2)}) %collective-permute-start.11) | collective-permute-done | bytes 65568 | tf_op jit(solution)/shard_map/ppermute | solution.py:501
  107.4 1.1 copy-done.1
  108.5 2.3 %line.1 = bf16[8,24,512]{2,1,0:T(8,128)(2,1)} custom-call(f32[96,512]{1,0:T(8,128)} %convert_reduce_fusion.early_ref, bf16[16,80,512]{2,1,0:T(8,128)(2,1)} %copy-done.1, s32[1]{0:T(128)} %bitcast.11.line_ref), custom_call_target="tpu_custom_call" | custom-call | flops 1000000000 | bytes 4000000 | tf_op jit(solution)/shard_map/line/pallas_call | solution.py:661
  110.8 5.7 %all-to-all-start.2 = ((bf16[8,24,512]{2,1,0:T(8,128)(2,1)}), bf16[8,24,512]{2,1,0:T(8,128)(2,1)S(1)}, u32[]{:S(2)}, u32[]{:S(2)}) async-start(bf16[8,24,512]{2,1,0:T(8,128)(2,1)} %line.1), calls=%async_computation.2 | async-start | bytes 393216 | tf_op jit(solution)/shard_map/all_to_all | solution.py:496
  116.6 1.3 collective-permute-start.15
  117.8 3.0 %collective-permute-done.15 = f32[128,128]{1,0:T(8,128)S(1)} collective-permute-done((f32[128,128]{1,0:T(8,128)S(1)}, f32[128,128]{1,0:T(8,128)S(1)}, u32[]{:S(2)}, u32[]{:S(2)}) %collective-permute-start.15) | collective-permute-done | bytes 65568 | tf_op jit(solution)/shard_map/ppermute | solution.py:501
  120.8 3.2 %collective-permute-start.16 = (f32[128,128]{1,0:T(8,128)S(1)}, f32[128,128]{1,0:T(8,128)S(1)}, u32[]{:S(2)}, u32[]{:S(2)}) collective-permute-start(f32[128,128]{1,0:T(8,128)S(1)} %add.51.small_ref), channel_id=1, source_target_pairs={{0,16},{16,0},{1,17},{17,1},{2,18},{18,2},{3,19},{19,3},{4,20},{20... | collective-permute-start | bytes 196616 | tf_op jit(solution)/shard_map/ppermute | solution.py:671
  124.1 2.6 %collective-permute-done.16.others_ref = f32[128,128]{1,0:T(8,128)S(1)} collective-permute-done((f32[128,128]{1,0:T(8,128)S(1)}, f32[128,128]{1,0:T(8,128)S(1)}, u32[]{:S(2)}, u32[]{:S(2)}) %collective-permute-start.16) | collective-permute-done | bytes 65568 | tf_op jit(solution)/shard_map/ppermute | solution.py:671
  126.7 0.6 copy-done.13
  127.3 0.7 copy-done.3
  128.0 1.6 %finish.1 = (f32[4096]{0:T(1024)}, f32[4096]{0:T(1024)}, f32[3072]{0:T(1024)}, f32[1024]{0:T(1024)}, f32[8,512]{1,0:T(8,128)}, /*index=5*/f32[2048]{0:T(1024)}, ...) custom-call(bf16[8,24,512]{2,1,0:T(8,128)(2,1)} %copy-done.3, f32[128,128]{1,0:T(8,128)} %copy-done.5, f32[128,128]{1,0:T(8,128)} %copy-done.13), custom_call_target="tpu_custom_call" | custom-call | flops 500000000 | bytes 2000000 | tf_op jit(solution)/shard_map/finish/pallas_call | solution.py:675
  (49 shorter events, 0.7 us)
Async XLA Ops:
  1.7 9.2 %collective-permute-start = (bf16[2,8,8,512]{3,2,1,0:T(8,128)(2,1)S(1)}, bf16[2,8,8,512]{3,2,1,0:T(8,128)(2,1)S(1)}, u32[]{:S(2)}, u32[]{:S(2)}) collective-permute-start(bf16[2,8,8,512]{3,2,1,0:T(8,128)(2,1)S(1)} %pad_maximum_fusion.2), channel_id=1, source_target_pairs={{0,240},{1,241},{2,242},{3,243},{4,244},{5,245},{6,246},{7,247},{8... | collective-permute-start | bytes 393224 | tf_op jit(solution)/shard_map/ppermute | solution.py:484
  4.5 6.3 %collective-permute-start.1 = (bf16[2,8,8,512]{3,2,1,0:T(8,128)(2,1)S(1)}, bf16[2,8,8,512]{3,2,1,0:T(8,128)(2,1)S(1)}, u32[]{:S(2)}, u32[]{:S(2)}) collective-permute-start(bf16[2,8,8,512]{3,2,1,0:T(8,128)(2,1)S(1)} %pad_maximum_fusion.3), channel_id=1, source_target_pairs={{0,15},{1,0},{2,1},{3,2},{4,3},{5,4},{6,5},{7,6},{8,7},{9,8},{10,9... | collective-permute-start | bytes 393224 | tf_op jit(solution)/shard_map/ppermute | solution.py:484
  6.7 6.9 %collective-permute-start.2 = (bf16[2,8,8,512]{3,2,1,0:T(8,128)(2,1)S(1)}, bf16[2,8,8,512]{3,2,1,0:T(8,128)(2,1)S(1)}, u32[]{:S(2)}, u32[]{:S(2)}) collective-permute-start(bf16[2,8,8,512]{3,2,1,0:T(8,128)(2,1)S(1)} %pad_maximum_fusion.4), channel_id=1, source_target_pairs={{0,255},{1,240},{2,241},{3,242},{4,243},{5,244},{6,245},{7,246},{8... | collective-permute-start | bytes 393224 | tf_op jit(solution)/shard_map/ppermute | solution.py:484
  10.9 2.7 %copy-start.7 = (bf16[2,8,8,512]{3,2,1,0:T(8,128)(2,1)}, bf16[2,8,8,512]{3,2,1,0:T(8,128)(2,1)S(1)}, u32[]{:S(2)}) copy-start(bf16[2,8,8,512]{3,2,1,0:T(8,128)(2,1)S(1)} %collective-permute-done.down_ref) | copy-start | bytes 393220
  10.9 2.7 %copy-start.8 = (bf16[2,8,8,512]{3,2,1,0:T(8,128)(2,1)}, bf16[2,8,8,512]{3,2,1,0:T(8,128)(2,1)S(1)}, u32[]{:S(2)}) copy-start(bf16[2,8,8,512]{3,2,1,0:T(8,128)(2,1)S(1)} %collective-permute-done.1.right_ref) | copy-start | bytes 393220
  13.6 0.6 copy-start.9
  30.9 5.8 %copy-start = (bf16[2048,512]{1,0:T(8,128)(2,1)S(1)}, bf16[2048,512]{1,0:T(8,128)(2,1)}, u32[]{:S(2)}) copy-start(bf16[2048,512]{1,0:T(8,128)(2,1)} %get-tuple-element.74) | copy-start | bytes 6291460
  30.9 4.6 %collective-permute-start.3 = (bf16[2048,512]{1,0:T(8,128)(2,1)}, bf16[2048,512]{1,0:T(8,128)(2,1)S(1)}, u32[]{:S(2)}, u32[]{:S(2)}) collective-permute-start(bf16[2048,512]{1,0:T(8,128)(2,1)} %get-tuple-element.75), channel_id=1, source_target_pairs={{0,1},{1,0},{2,3},{3,2},{4,5},{5,4},{6,7},{7,6},{8,9},{9,8},{10,11... | collective-permute-start | bytes 6291464 | tf_op jit(solution)/shard_map/ppermute | solution.py:488
  38.5 32.9 %all-to-all-start = ((bf16[16,96,512]{2,1,0:T(8,128)(2,1)}), bf16[16,96,512]{2,1,0:T(8,128)(2,1)S(1)}, u32[]{:S(2)}, u32[]{:S(2)}) async-start(bf16[16,96,512]{2,1,0:T(8,128)(2,1)} %pad_maximum_fusion), calls=%async_computation | async-start | bytes 3145728 | tf_op jit(solution)/shard_map/all_to_all | solution.py:496
  45.6 15.0 %collective-permute-start.4 = (bf16[256,512]{1,0:T(8,128)(2,1)S(1)}, bf16[256,512]{1,0:T(8,128)(2,1)S(1)}, u32[]{:S(2)}, u32[]{:S(2)}) collective-permute-start(bf16[256,512]{1,0:T(8,128)(2,1)S(1)} %get-tuple-element.83), channel_id=1, source_target_pairs={{0,32},{32,0},{64,96},{96,64},{128,160},{160,128},{192,224},{224,1... | collective-permute-start | bytes 786440 | tf_op jit(solution)/shard_map/ppermute | solution.py:506
  60.6 3.9 %copy-start.4 = (f32[128,128]{1,0:T(8,128)S(1)}, f32[128,128]{1,0:T(8,128)}, u32[]{:S(2)}) copy-start(f32[128,128]{1,0:T(8,128)} %table.1) | copy-start | bytes 196612
  64.5 6.9 %collective-permute-start.5 = (bf16[1024,512]{1,0:T(8,128)(2,1)}, bf16[1024,512]{1,0:T(8,128)(2,1)}, u32[]{:S(2)}, u32[]{:S(2)}) collective-permute-start(bf16[1024,512]{1,0:T(8,128)(2,1)} %get-tuple-element.92), channel_id=1, source_target_pairs={{0,1},{1,0},{2,3},{3,2},{4,5},{5,4},{6,7},{7,6},{8,9},{9,8},{10,11... | collective-permute-start | bytes 3145736 | tf_op jit(solution)/shard_map/ppermute | solution.py:488
  64.5 2.4 %collective-permute-start.6 = (f32[128,128]{1,0:T(8,128)S(1)}, f32[128,128]{1,0:T(8,128)S(1)}, u32[]{:S(2)}, u32[]{:S(2)}) collective-permute-start(f32[128,128]{1,0:T(8,128)S(1)} %copy-done.4), channel_id=1, source_target_pairs={{0,1},{1,0},{2,3},{3,2},{4,5},{5,4},{6,7},{7,6},{8,9},{9,8},{10,11... | collective-permute-start | bytes 196616 | tf_op jit(solution)/shard_map/ppermute | solution.py:488
  65.1 6.3 %copy-start.2 = (bf16[1024,512]{1,0:T(8,128)(2,1)S(1)}, bf16[1024,512]{1,0:T(8,128)(2,1)}, u32[]{:S(2)}) copy-start(bf16[1024,512]{1,0:T(8,128)(2,1)} %get-tuple-element.102) | copy-start | bytes 3145732
  66.9 4.5 %collective-permute-start.7 = (f32[128,128]{1,0:T(8,128)S(1)}, f32[128,128]{1,0:T(8,128)S(1)}, u32[]{:S(2)}, u32[]{:S(2)}) collective-permute-start(f32[128,128]{1,0:T(8,128)S(1)} %add.43), channel_id=1, source_target_pairs={{0,32},{32,0},{64,96},{96,64},{128,160},{160,128},{192,224},{224,1... | collective-permute-start | bytes 196616 | tf_op jit(solution)/shard_map/ppermute | solution.py:501
  72.9 18.8 %copy-start.12 = (bf16[8,8,512]{2,1,0:T(8,128)(2,1)S(1)}, bf16[8,8,512]{2,1,0:T(8,128)(2,1)}, u32[]{:S(2)}) copy-start(bf16[8,8,512]{2,1,0:T(8,128)(2,1)} %get-tuple-element.107) | copy-start | bytes 196612
  72.9 19.3 %copy-start.11 = (bf16[8,8,512]{2,1,0:T(8,128)(2,1)S(1)}, bf16[8,8,512]{2,1,0:T(8,128)(2,1)}, u32[]{:S(2)}) copy-start(bf16[8,8,512]{2,1,0:T(8,128)(2,1)} %get-tuple-element.108) | copy-start | bytes 196612
  72.9 22.4 %copy-start.10 = (bf16[8,8,512]{2,1,0:T(8,128)(2,1)S(1)}, bf16[8,8,512]{2,1,0:T(8,128)(2,1)}, u32[]{:S(2)}) copy-start(bf16[8,8,512]{2,1,0:T(8,128)(2,1)} %get-tuple-element.109) | copy-start | bytes 196612
  74.2 30.2 %copy-start.6 = (bf16[8,8,512]{2,1,0:T(8,128)(2,1)S(1)}, bf16[8,8,512]{2,1,0:T(8,128)(2,1)}, u32[]{:S(2)}) copy-start(bf16[8,8,512]{2,1,0:T(8,128)(2,1)} %get-tuple-element.110) | copy-start | bytes 196612
  74.2 33.3 %all-to-all-start.1 = ((bf16[16,80,512]{2,1,0:T(8,128)(2,1)}), bf16[16,80,512]{2,1,0:T(8,128)(2,1)S(1)}, u32[]{:S(2)}, u32[]{:S(2)}) async-start(bf16[16,80,512]{2,1,0:T(8,128)(2,1)} %pad_maximum_fusion.1), calls=%async_computation.1 | async-start | bytes 2621440 | tf_op jit(solution)/shard_map/all_to_all | solution.py:496
  81.4 5.4 %collective-permute-start.8 = (f32[128,128]{1,0:T(8,128)S(1)}, f32[128,128]{1,0:T(8,128)S(1)}, u32[]{:S(2)}, u32[]{:S(2)}) collective-permute-start(f32[128,128]{1,0:T(8,128)S(1)} %add.44), channel_id=1, source_target_pairs={{0,64},{32,96},{64,0},{96,32},{128,192},{160,224},{192,128},{224,1... | collective-permute-start | bytes 196616 | tf_op jit(solution)/shard_map/ppermute | solution.py:501
  86.7 10.4 %collective-permute-start.9 = (f32[128,128]{1,0:T(8,128)S(1)}, f32[128,128]{1,0:T(8,128)S(1)}, u32[]{:S(2)}, u32[]{:S(2)}) collective-permute-start(f32[128,128]{1,0:T(8,128)S(1)} %add.47), channel_id=1, source_target_pairs={{0,128},{32,160},{64,192},{96,224},{128,0},{160,32},{192,64},{224,... | collective-permute-start | bytes 196616 | tf_op jit(solution)/shard_map/ppermute | solution.py:501
  91.7 12.6 %collective-permute-start.12 = (bf16[8,8,512]{2,1,0:T(8,128)(2,1)S(1)}, bf16[8,8,512]{2,1,0:T(8,128)(2,1)S(1)}, u32[]{:S(2)}, u32[]{:S(2)}) collective-permute-start(bf16[8,8,512]{2,1,0:T(8,128)(2,1)S(1)} %copy-done.12), channel_id=1, source_target_pairs={{0,17},{1,18},{2,19},{3,20},{4,21},{5,22},{6,23},{7,24},{8,25},{9,... | collective-permute-start | bytes 196616 | tf_op jit(solution)/shard_map/ppermute | solution.py:484
  92.3 12.1 %collective-permute-start.13 = (bf16[8,8,512]{2,1,0:T(8,128)(2,1)S(1)}, bf16[8,8,512]{2,1,0:T(8,128)(2,1)S(1)}, u32[]{:S(2)}, u32[]{:S(2)}) collective-permute-start(bf16[8,8,512]{2,1,0:T(8,128)(2,1)S(1)} %copy-done.11), channel_id=1, source_target_pairs={{0,16},{1,17},{2,18},{3,19},{4,20},{5,21},{6,22},{7,23},{8,24},{9,... | collective-permute-start | bytes 196616 | tf_op jit(solution)/shard_map/ppermute | solution.py:484
  95.3 9.0 %collective-permute-start.14 = (bf16[8,8,512]{2,1,0:T(8,128)(2,1)S(1)}, bf16[8,8,512]{2,1,0:T(8,128)(2,1)S(1)}, u32[]{:S(2)}, u32[]{:S(2)}) collective-permute-start(bf16[8,8,512]{2,1,0:T(8,128)(2,1)S(1)} %copy-done.10), channel_id=1, source_target_pairs={{0,1},{1,2},{2,3},{3,4},{4,5},{5,6},{6,7},{7,8},{8,9},{9,10},{10,1... | collective-permute-start | bytes 196616 | tf_op jit(solution)/shard_map/ppermute | solution.py:484
  97.2 4.4 %collective-permute-start.10 = (f32[128,128]{1,0:T(8,128)S(1)}, f32[128,128]{1,0:T(8,128)S(1)}, u32[]{:S(2)}, u32[]{:S(2)}) collective-permute-start(f32[128,128]{1,0:T(8,128)S(1)} %add.48), channel_id=1, source_target_pairs={{0,2},{2,0},{4,6},{6,4},{1,3},{3,1},{5,7},{7,5},{8,10},{10,8},{12,... | collective-permute-start | bytes 196616 | tf_op jit(solution)/shard_map/ppermute | solution.py:501
  101.5 5.9 %collective-permute-start.11 = (f32[128,128]{1,0:T(8,128)S(1)}, f32[128,128]{1,0:T(8,128)S(1)}, u32[]{:S(2)}, u32[]{:S(2)}) collective-permute-start(f32[128,128]{1,0:T(8,128)S(1)} %add.49), channel_id=1, source_target_pairs={{0,4},{2,6},{4,0},{6,2},{1,5},{3,7},{5,1},{7,3},{8,12},{10,14},{12... | collective-permute-start | bytes 196616 | tf_op jit(solution)/shard_map/ppermute | solution.py:501
  107.4 1.1 copy-start.1
  110.8 15.9 %all-to-all-start.2 = ((bf16[8,24,512]{2,1,0:T(8,128)(2,1)}), bf16[8,24,512]{2,1,0:T(8,128)(2,1)S(1)}, u32[]{:S(2)}, u32[]{:S(2)}) async-start(bf16[8,24,512]{2,1,0:T(8,128)(2,1)} %line.1), calls=%async_computation.2 | async-start | bytes 393216 | tf_op jit(solution)/shard_map/all_to_all | solution.py:496
  116.6 4.3 %collective-permute-start.15 = (f32[128,128]{1,0:T(8,128)S(1)}, f32[128,128]{1,0:T(8,128)S(1)}, u32[]{:S(2)}, u32[]{:S(2)}) collective-permute-start(f32[128,128]{1,0:T(8,128)S(1)} %add.50), channel_id=1, source_target_pairs={{0,8},{8,0},{1,9},{9,1},{2,10},{10,2},{3,11},{11,3},{4,12},{12,4},... | collective-permute-start | bytes 196616 | tf_op jit(solution)/shard_map/ppermute | solution.py:501
  120.8 5.9 %copy-start.5 = (f32[128,128]{1,0:T(8,128)}, f32[128,128]{1,0:T(8,128)S(1)}, u32[]{:S(2)}) copy-start(f32[128,128]{1,0:T(8,128)S(1)} %add.51.small_ref) | copy-start | bytes 196612
  120.8 5.9 %collective-permute-start.16 = (f32[128,128]{1,0:T(8,128)S(1)}, f32[128,128]{1,0:T(8,128)S(1)}, u32[]{:S(2)}, u32[]{:S(2)}) collective-permute-start(f32[128,128]{1,0:T(8,128)S(1)} %add.51.small_ref), channel_id=1, source_target_pairs={{0,16},{16,0},{1,17},{17,1},{2,18},{18,2},{3,19},{19,3},{4,20},{20... | collective-permute-start | bytes 196616 | tf_op jit(solution)/shard_map/ppermute | solution.py:671
  126.7 0.6 copy-start.13
  127.3 0.7 copy-start.3
